TPU v7x, 32 devices: a whole 2x2x4 slice. The times are simulated.
32 devices in a mesh: ens: 4 (over z), polar: 2 (over core), azimuth: 4 (over y, x).
Axes of the slice: x: 2, y: 2, z: 4, core: 2. Of those that a mesh axis runs over, the one named last changes fastest.
Arguments:
- fields: bfloat16 [4, 16, 1440, 256], P('ens', 'polar', 'azimuth'), may hold values from -6 to 6
- basis_spectra: bfloat16 [9, 8, 5, 720], P(None, 'polar'), may hold values from -3 to 3
- support: int32 [8, 2], P('polar'), may hold values from 0 to 4, as said below
- weights: bfloat16 [9, 256, 256], replicated, may hold values from -0.125 to 0.125
- out_grad: bfloat16 [4, 8, 720, 256], P('ens', 'polar', 'azimuth'), may hold values from -6 to 6
Outputs:
- conv_out: bfloat16 [4, 8, 720, 256], P('ens', 'polar', 'azimuth')
- field_grad: bfloat16 [4, 16, 1440, 256], P('ens', 'polar', 'azimuth')
- weight_grad: float32 [9, 256, 256], P(None, 'azimuth')
Inputs may be any that keep to these rules, and one draw needn't show every extreme that they name: Row o uses window rows support[o, 0] to support[o, 1]; support[o, 0] <= 2 <= support[o, 1]; rows o with o mod 4 equal to 0 or 3 use the whole window.
All inputs are finite; a program needn't handle non-finite values.
Results may differ from a plain program's by a relative error of at most 0.02.
Values may be sent and summed in bfloat16 or wider, within the bound.
A program may use at most 64 MiB of HBM per device.

v0:
```python
import math

import jax
import jax.numpy as jnp
import ml_dtypes
import numpy as np
from jax import lax
from jax.experimental import pallas as pl
from jax.experimental.pallas import tpu as pltpu
from jax.sharding import PartitionSpec as P

LANES = 128
ROWS = 16
F32 = jnp.float32
BF16 = jnp.bfloat16
NT = (((1,), (1,)), ((), ()))


def padded_modes(modes):
    return -(-modes // LANES) * LANES


def make_tables(width_in, width_out, shares):
    modes = width_out // 2
    wide = padded_modes(modes)
    frequency = np.arange(modes)
    phases = np.arange(width_in)[:, None] * frequency[None, :] % width_in
    angles = (phases.astype(np.float32) * np.float32(2.0 * math.pi / width_in)).astype(np.float64)
    forward = np.zeros((width_in, 2, wide), np.float32)
    forward[:, 0, :modes] = np.cos(angles)
    forward[:, 1, :modes] = -np.sin(angles)
    phases = frequency[:, None] * np.arange(width_out)[None, :] % width_out
    angles = (phases.astype(np.float32) * np.float32(2.0 * math.pi / width_out)).astype(np.float64)
    factors = (np.where(frequency == 0, 1.0, 2.0) / width_in)[:, None]
    inverse = np.zeros((2, wide, width_out), np.float32)
    inverse[0, :modes] = factors * np.cos(angles)
    inverse[1, :modes] = -factors * np.sin(angles)
    forward = forward.reshape(shares, width_in // shares, 2 * wide).astype(ml_dtypes.bfloat16)
    inverse = inverse.reshape(2 * wide, shares, width_out // shares).astype(ml_dtypes.bfloat16)
    return (
        forward,
        np.ascontiguousarray(forward.transpose(0, 2, 1)),
        np.ascontiguousarray(inverse.transpose(1, 0, 2)),
        np.ascontiguousarray(inverse.transpose(1, 2, 0)),
    )


def filter_rows(basis, support):
    k, outs, window, columns = basis.shape
    modes = columns // 2
    at = jnp.arange(window, dtype=jnp.int32)
    inside = (at[None, :] >= support[:, 0:1]) & (at[None, :] <= support[:, 1:2])
    masked = jnp.where(inside[None, :, :, None], basis, jnp.zeros_like(basis)).astype(F32)
    masked = masked.reshape(k, outs, 2 * window, modes).transpose(1, 0, 2, 3)
    extra = -(2 * window) % 8
    return jnp.pad(masked, ((0, 0), (0, 0), (0, extra), (0, padded_modes(modes) - modes)))


def whole(shape):
    return pl.BlockSpec(shape, lambda i: (0,) * len(shape))


def params():
    return pltpu.CompilerParams(
        dimension_semantics=("arbitrary",), vmem_limit_bytes=40 * 1024 * 1024
    )


def cost(flops, moved):
    return pl.CostEstimate(flops=int(flops), bytes_accessed=int(moved), transcendentals=0)


def back_kernel(window, og_ref, inv_ref, w_ref, mk_ref, gs_ref, sg_ref, mg_ref):
    o = pl.program_id(0)
    shares = og_ref.shape[0]
    taps, share, columns = mg_ref.shape
    wide = columns // 2
    block = min(ROWS, share)

    @pl.when(o == 0)
    def _():
        sg_ref[...] = jnp.zeros_like(sg_ref)

    total = jnp.dot(inv_ref[0], og_ref[0, 0], preferred_element_type=F32)
    for s in range(1, shares):
        total += jnp.dot(inv_ref[s], og_ref[s, 0], preferred_element_type=F32)
    gs = total.astype(BF16)
    gs_ref[0] = gs
    for k in range(taps):
        mg_ref[k] = lax.dot_general(w_ref[k], gs, NT, preferred_element_type=F32)

    for at in range(0, wide, LANES):
        re = slice(at, at + LANES)
        im = slice(wide + at, wide + at + LANES)

        @pl.loop(0, share // block)
        def _(c):
            rows = pl.ds(pl.multiple_of(c * block, block), block)
            acc = [[None, None] for _ in range(window)]
            for k in range(taps):
                gr = mg_ref[k, rows, re]
                gi = mg_ref[k, rows, im]
                for j in range(window):
                    pr = mk_ref[0, k, 2 * j : 2 * j + 1, re]
                    pi = mk_ref[0, k, 2 * j + 1 : 2 * j + 2, re]
                    br = pr * gr + pi * gi
                    bi = pr * gi - pi * gr
                    acc[j][0] = br if k == 0 else acc[j][0] + br
                    acc[j][1] = bi if k == 0 else acc[j][1] + bi
            for j in range(window):
                sg_ref[2 * o + j, rows, re] += acc[j][0]
                sg_ref[2 * o + j, rows, im] += acc[j][1]


def backward_spectra(gathered, inverse, weights, filters, window, rows_total):
    shares, outs, part, d = gathered.shape
    taps, share, _ = weights.shape
    columns = inverse.shape[1]
    return pl.pallas_call(
        lambda *refs: back_kernel(window, *refs),
        grid=(outs,),
        in_specs=[
            pl.BlockSpec((shares, 1, part, d), lambda i: (0, i, 0, 0)),
            whole(inverse.shape),
            whole(weights.shape),
            pl.BlockSpec((1,) + filters.shape[1:], lambda i: (i, 0, 0, 0)),
        ],
        out_specs=[
            pl.BlockSpec((1, columns, d), lambda i: (i, 0, 0)),
            whole((rows_total, share, columns)),
        ],
        out_shape=[
            jax.ShapeDtypeStruct((outs, columns, d), BF16),
            jax.ShapeDtypeStruct((rows_total, share, columns), F32),
        ],
        scratch_shapes=[pltpu.VMEM((taps, share, columns), F32)],
        compiler_params=params(),
        cost_estimate=cost(2e10, 1e7),
    )(gathered, inverse, weights, filters)


def field_grad_kernel(sg_ref, low_ref, high_ref, table_ref, out_ref):
    i = pl.program_id(0)
    last = pl.num_programs(0) - 1
    rows, share, columns = sg_ref.shape
    low = jnp.where(i == 0, low_ref[...].astype(F32), 0.0)
    high = jnp.where(i == last, high_ref[...].astype(F32), 0.0)
    value = (sg_ref[...] + low + high).astype(BF16).reshape(rows * share, columns)
    for s in range(table_ref.shape[0]):
        piece = jnp.dot(value, table_ref[s], preferred_element_type=F32)
        out_ref[s] = piece.astype(BF16).reshape(rows, share, piece.shape[1])


def field_gradient(sg, low, high, table):
    rim, share, columns = low.shape
    rows = sg.shape[0] - 2 * rim
    shares, _, part = table.shape
    return pl.pallas_call(
        field_grad_kernel,
        grid=(rows // rim,),
        in_specs=[
            pl.BlockSpec((rim, share, columns), lambda i: (i + 1, 0, 0)),
            whole(low.shape),
            whole(high.shape),
            whole(table.shape),
        ],
        out_specs=pl.BlockSpec((shares, rim, share, part), lambda i: (0, i, 0, 0)),
        out_shape=jax.ShapeDtypeStruct((shares, rows, share, part), BF16),
        compiler_params=params(),
        cost_estimate=cost(5e9, 6e6),
    )(sg, low, high, table)


def spectra_kernel(x_ref, table_ref, out_ref):
    shares, rows, share, part = x_ref.shape
    total = None
    for s in range(shares):
        term = jnp.dot(
            x_ref[s].reshape(rows * share, part), table_ref[s], preferred_element_type=F32
        )
        total = term if total is None else total + term
    out_ref[...] = total.reshape(out_ref.shape)


def input_spectra(x, table, rim):
    shares, rows, share, part = x.shape
    columns = table.shape[2]
    return pl.pallas_call(
        spectra_kernel,
        grid=(rows // rim,),
        in_specs=[
            pl.BlockSpec((shares, rim, share, part), lambda i: (0, i, 0, 0)),
            whole(table.shape),
        ],
        out_specs=pl.BlockSpec((rim, share, columns), lambda i: (i, 0, 0)),
        out_shape=jax.ShapeDtypeStruct((rows, share, columns), F32),
        compiler_params=params(),
        cost_estimate=cost(5e9, 6e6),
    )(x, table)


def mix_kernel(window, x_ref, low_ref, high_ref, mk_ref, gs_ref, wt_ref, inv_ref,
               conv_ref, wg_ref, ext_ref, mixed_ref, total_ref):
    o = pl.program_id(0)
    rows, share, columns = x_ref.shape
    rim = low_ref.shape[0]
    taps = mixed_ref.shape[0]
    wide = columns // 2
    block = min(ROWS, share)

    @pl.when(o == 0)
    def _():
        ext_ref[0:rim] = low_ref[...].astype(F32)
        ext_ref[rim : rim + rows] = x_ref[...]
        ext_ref[rim + rows :] = high_ref[...].astype(F32)
        total_ref[...] = jnp.zeros_like(total_ref)

    for at in range(0, wide, LANES):
        re = slice(at, at + LANES)
        im = slice(wide + at, wide + at + LANES)

        @pl.loop(0, share // block)
        def _(c):
            here = pl.ds(pl.multiple_of(c * block, block), block)
            xr = [ext_ref[2 * o + j, here, re] for j in range(window)]
            xi = [ext_ref[2 * o + j, here, im] for j in range(window)]
            for k in range(taps):
                mr = mi = None
                for j in range(window):
                    pr = mk_ref[0, k, 2 * j : 2 * j + 1, re]
                    pi = mk_ref[0, k, 2 * j + 1 : 2 * j + 2, re]
                    tr = pr * xr[j] - pi * xi[j]
                    ti = pr * xi[j] + pi * xr[j]
                    mr = tr if j == 0 else mr + tr
                    mi = ti if j == 0 else mi + ti
                mixed_ref[k, here, re] = mr.astype(BF16)
                mixed_ref[k, here, im] = mi.astype(BF16)

    mixed = mixed_ref[...].reshape(taps * share, columns)
    total_ref[...] += jnp.dot(mixed, gs_ref[0], preferred_element_type=F32)
    spec = jnp.dot(wt_ref[...], mixed, preferred_element_type=F32).astype(BF16)
    for s in range(inv_ref.shape[0]):
        conv_ref[s, 0] = lax.dot_general(
            inv_ref[s], spec, NT, preferred_element_type=F32
        ).astype(BF16)

    @pl.when(o == pl.num_programs(0) - 1)
    def _():
        wg_ref[...] = total_ref[...].astype(BF16)


def mix(x, low, high, filters, gs, weights_t, inverse_t, window):
    rows, share, columns = x.shape
    rim = low.shape[0]
    outs, taps = filters.shape[:2]
    d = gs.shape[2]
    shares, part, _ = inverse_t.shape
    return pl.pallas_call(
        lambda *refs: mix_kernel(window, *refs),
        grid=(outs,),
        in_specs=[
            whole(x.shape),
            whole(low.shape),
            whole(high.shape),
            pl.BlockSpec((1,) + filters.shape[1:], lambda i: (i, 0, 0, 0)),
            pl.BlockSpec((1, columns, d), lambda i: (i, 0, 0)),
            whole(weights_t.shape),
            whole(inverse_t.shape),
        ],
        out_specs=[
            pl.BlockSpec((shares, 1, part, d), lambda i: (0, i, 0, 0)),
            whole((taps * share, d)),
        ],
        out_shape=[
            jax.ShapeDtypeStruct((shares, outs, part, d), BF16),
            jax.ShapeDtypeStruct((taps * share, d), BF16),
        ],
        scratch_shapes=[
            pltpu.VMEM((rows + 2 * rim, share, columns), F32),
            pltpu.VMEM((taps, share, columns), BF16),
            pltpu.VMEM((taps * share, d), F32),
        ],
        compiler_params=params(),
        cost_estimate=cost(2e10, 1e7),
    )(x, low, high, filters, gs, weights_t, inverse_t)


def to_neighbours(first, last):
    count = lax.axis_size("polar")
    up = [(i, i + 1) for i in range(count - 1)]
    down = [(i + 1, i) for i in range(count - 1)]
    return lax.ppermute(last, "polar", up), lax.ppermute(first, "polar", down)


def local(fields, basis_spectra, support, weights, out_grad):
    shares = lax.axis_size("azimuth")
    window = basis_spectra.shape[2]
    margin = window // 2
    _, rows, part, channels = fields.shape
    share = channels // shares
    taps, _, d = weights.shape
    forward, forward_t, inverse, inverse_t = make_tables(
        part * shares, out_grad.shape[2] * shares, shares
    )
    gathered = lax.all_gather(out_grad[0], "azimuth", axis=0)
    pieces = fields[0].reshape(rows, part, shares, share).transpose(2, 0, 3, 1)
    spread = lax.all_to_all(pieces, "azimuth", 0, 0)
    filters = filter_rows(basis_spectra, support)
    own = lax.dynamic_slice_in_dim(weights, lax.axis_index("azimuth") * share, share, 1)
    own_t = own.reshape(taps * share, d).T

    gs, sg = backward_spectra(
        gathered, jnp.asarray(inverse), own, filters, window, rows + 2 * margin
    )
    low, high = to_neighbours(sg[:margin].astype(BF16), sg[margin + rows :].astype(BF16))
    grad_pieces = field_gradient(sg, low, high, jnp.asarray(forward_t))
    grad_back = lax.all_to_all(grad_pieces, "azimuth", 0, 0)

    x = input_spectra(spread, jnp.asarray(forward), margin)
    low, high = to_neighbours(x[:margin].astype(BF16), x[rows - margin :].astype(BF16))
    conv_parts, wg = mix(x, low, high, filters, gs, own_t, jnp.asarray(inverse_t), window)

    axes = ("ens", "polar")
    count = lax.axis_size("ens") * lax.axis_size("polar")
    terms = lax.all_to_all(wg.reshape(count, -1, d), axes, 0, 0)
    conv_terms = lax.all_to_all(conv_parts, "azimuth", 0, 0)
    summed = jnp.sum(terms.astype(F32), axis=0).astype(BF16)
    weight_grad = lax.all_gather(summed, axes, axis=0, tiled=True)
    weight_grad = weight_grad.reshape(taps, share, d).astype(F32)
    conv_out = jnp.sum(conv_terms.astype(F32), axis=0).astype(BF16)
    field_grad = grad_back.transpose(1, 3, 0, 2).reshape(rows, part, channels)
    return (conv_out[None], field_grad[None], weight_grad)


def solution(mesh):
    placed = (
        P("ens", "polar", "azimuth", None),
        P(None, "polar", None, None),
        P("polar", None),
        P(),
        P("ens", "polar", "azimuth", None),
    )
    return jax.shard_map(
        local,
        mesh=mesh,
        in_specs=placed,
        out_specs=(
            P("ens", "polar", "azimuth", None),
            P("ens", "polar", "azimuth", None),
            P(None, "azimuth", None),
        ),
        check_vma=False,
    )
```

profile of v0, /device:TPU:0, one launch (start us, length us, event | category | flops | bytes accessed | tf_op | source)
XLA Modules:
  0.0 156.2 jit_solution(10920254605589308510)
XLA Ops:
  7.2 0.0 copy-start
  7.2 0.0 all-gather.2.cloned.1.call-start
  7.2 0.7 all-gather.2.cloned.1.call-update
  7.9 1.9 %copy.23 = bf16[1,8,360,256]{2,3,1,0:T(8,128)(2,1)S(1)} copy(bf16[1,8,360,256]{3,2,1,0:T(8,128)(2,1)} %param.9) | data formatting | bytes 2949120 | tf_op args[0]
  9.8 1.4 copy.39
  11.2 5.3 %all-to-all-start = ((bf16[4,8,64,360]{3,2,1,0:T(8,128)(2,1)}), bf16[4,8,64,360]{3,2,1,0:T(8,128)(2,1)S(1)}, u32[]{:S(2)}, u32[]{:S(2)}) async-start(bf16[4,8,64,360]{3,2,1,0:T(8,128)(2,1)} %bitcast.24), calls=%async_computation | async-start | bytes 3145728 | tf_op jit(solution)/shard_map/all_to_all | solution.py:307
  16.5 0.2 broadcast_select_fusion
  16.7 1.2 reshape.70
  18.0 0.9 copy.28
  18.9 2.0 %pad_convert_fusion.refs_3_ = f32[4,9,16,384]{3,2,1,0:T(8,128)} fusion(bf16[4,9,10,360]{3,2,1,0:T(8,128)(2,1)} %bitcast.28), kind=kLoop, calls=%fused_computation.1 | loop fusion | flops 221184 | bytes 1143936 | tf_op jit(solution)/shard_map/jit(_pad)/pad | solution.py:56
  20.9 18.8 %all-to-all-done.x_ref = bf16[4,8,64,360]{3,2,1,0:T(8,128)(2,1)S(1)} async-done(((bf16[4,8,64,360]{3,2,1,0:T(8,128)(2,1)}), bf16[4,8,64,360]{3,2,1,0:T(8,128)(2,1)S(1)}, u32[]{:S(2)}, u32[]{:S(2)}) %all-to-all-start) | async-done | bytes 1474592 | tf_op jit(solution)/shard_map/all_to_all | solution.py:307
  39.7 1.6 %copy-done.12 = bf16[4,360,768]{2,1,0:T(8,128)(2,1)S(1)} copy-done((bf16[4,360,768]{2,1,0:T(8,128)(2,1)S(1)}, bf16[4,360,768]{2,1,0:T(8,128)(2,1)}, u32[]{:S(2)}) %copy-start.12) | copy-done | bytes 2211864
  41.3 2.4 %shard_map.112.refs_0_ = f32[8,64,768]{2,1,0:T(8,128)S(1)} custom-call(bf16[4,8,64,360]{3,2,1,0:T(8,128)(2,1)S(1)} %all-to-all-done.x_ref, bf16[4,360,768]{2,1,0:T(8,128)(2,1)S(1)} %copy-done.12), custom_call_target="tpu_custom_call" | custom-call | flops 5000000000 | bytes 6000000 | tf_op jit(solution)/shard_map/pallas_call | solution.py:188
  43.8 0.1 convert.15
  43.9 0.9 fusion.2
  44.8 0.3 copy-done.1
  45.1 2.0 %collective-permute-start = (bf16[2,64,768]{2,1,0:T(8,128)(2,1)}, bf16[2,64,768]{2,1,0:T(8,128)(2,1)}, u32[]{:S(2)}, u32[]{:S(2)}) collective-permute-start(bf16[2,64,768]{2,1,0:T(8,128)(2,1)} %get-tuple-element.20), channel_id=1, source_target_pairs={{0,4},{1,5},{2,6},{3,7},{8,12},{9,13},{10,14},{11,15},{16,20},{17,... | collective-permute-start | bytes 589832 | tf_op jit(solution)/shard_map/ppermute | solution.py:292
  47.1 1.3 collective-permute-start.1
  48.3 3.2 %all-gather.2.cloned.1.call-done = bf16[4,4,180,256]{3,1,2,0:T(4,128)(2,1)} async-done(((bf16[1,4,180,256]{3,1,2,0:T(4,128)(2,1)}), bf16[4,4,180,256]{3,1,2,0:T(4,128)(2,1)}) %all-gather.2.cloned.1.call-update) | async-done | bytes 1474576 | tf_op jit(solution)/shard_map/all_gather | solution.py:305
  51.5 1.6 %copy.27.refs_0_ = bf16[4,4,180,256]{3,2,1,0:T(8,128)(2,1)S(1)} copy(bf16[4,4,180,256]{3,1,2,0:T(4,128)(2,1)} %all-gather.2.cloned.1.call-done) | data formatting | bytes 2949120 | tf_op jit(solution)/shard_map/all_gather | solution.py:305
  53.1 1.0 copy-done.6
  54.1 1.2 copy-done.7
  55.2 1.4 copy-done.13
  56.7 14.7 %shard_map.113 = (bf16[4,768,256]{2,1,0:T(8,128)(2,1)S(1)}, f32[12,64,768]{2,1,0:T(8,128)S(1)}) custom-call(bf16[4,4,180,256]{3,2,1,0:T(8,128)(2,1)S(1)} %copy.27.refs_0_, bf16[4,768,180]{2,1,0:T(8,128)(2,1)S(1)} %copy-done.13, bf16[9,64,256]{2,1,0:T(8,128)(2,1)S(1)} %copy-done.6, f32[4,9,16,384]{3,2,1,0:T(8,128)S(1)} %copy-done.7), custom_call_target="tpu_custom_call" | custom-call | flops 20000000000 | bytes 10000000 | tf_op jit(solution)/shard_map/pallas_call | solution.py:119
  71.4 0.0 collective-permute-done.refs_1_
  71.4 11.6 %shard_map.114 = (bf16[4,4,180,256]{3,2,1,0:T(8,128)(2,1)S(1)}, bf16[576,256]{1,0:T(8,128)(2,1)S(1)}) custom-call(f32[8,64,768]{2,1,0:T(8,128)S(1)} %copy-done.2, bf16[2,64,768]{2,1,0:T(8,128)(2,1)} %collective-permute-done.refs_1_, bf16[2,64,768]{2,1,0:T(8,128)(2,1)} %collective-permute-done.1.refs_2_, f32[4,9,16,384]{3,2,1,0:T(8,128)S(1)} %copy-done.8, ...), custom_call_target="tpu_custom_call" | custom-call | flops 20000000000 | bytes 10000000 | tf_op jit(solution)/shard_map/pallas_call | solution.py:258
  83.0 1.1 copy-done.4
  84.1 0.7 copy-done.10
  84.9 4.6 %all-to-all-start.3 = ((bf16[8,72,256]{2,1,0:T(8,128)(2,1)}), bf16[8,72,256]{2,1,0:T(8,128)(2,1)}, u32[]{:S(2)}, u32[]{:S(2)}) async-start(bf16[8,72,256]{2,1,0:T(8,128)(2,1)} %bitcast.23), calls=%async_computation.3 | async-start | bytes 589824 | tf_op jit(solution)/shard_map/all_to_all | solution.py:325
  89.5 3.1 %copy.29 = bf16[4,4,180,256]{3,1,2,0:T(4,128)(2,1)} copy(bf16[4,4,180,256]{3,2,1,0:T(8,128)(2,1)} %copy-done.4) | data formatting | bytes 2949120 | tf_op jit(solution)/shard_map/pallas_call | solution.py:258
  92.5 7.5 %all-to-all-done.3 = bf16[8,72,256]{2,1,0:T(8,128)(2,1)} async-done(((bf16[8,72,256]{2,1,0:T(8,128)(2,1)}), bf16[8,72,256]{2,1,0:T(8,128)(2,1)}, u32[]{:S(2)}, u32[]{:S(2)}) %all-to-all-start.3) | async-done | bytes 294944 | tf_op jit(solution)/shard_map/all_to_all | solution.py:325
  100.0 4.4 %all-to-all-start.1 = ((bf16[4,4,180,256]{3,1,2,0:T(4,128)(2,1)}), bf16[4,4,180,256]{3,1,2,0:T(4,128)(2,1)}, u32[]{:S(2)}, u32[]{:S(2)}) async-start(bf16[4,4,180,256]{3,1,2,0:T(4,128)(2,1)} %copy.29), calls=%async_computation.1 | async-start | bytes 2949120 | tf_op jit(solution)/shard_map/all_to_all | solution.py:326
  104.4 0.0 copy-start.11
  104.4 0.1 convert.16
  104.6 1.5 collective-permute-start.2
  106.0 1.3 collective-permute-start.3
  107.4 2.0 %collective-permute-done.3.high_ref = bf16[2,64,768]{2,1,0:T(8,128)(2,1)S(1)} collective-permute-done((bf16[2,64,768]{2,1,0:T(8,128)(2,1)S(1)}, bf16[2,64,768]{2,1,0:T(8,128)(2,1)S(1)}, u32[]{:S(2)}, u32[]{:S(2)}) %collective-permute-start.3) | collective-permute-done | bytes 196640 | tf_op jit(solution)/shard_map/ppermute | solution.py:292
  109.4 2.4 %shard_map.115 = bf16[4,8,64,360]{3,2,1,0:T(8,128)(2,1)S(1)} custom-call(f32[12,64,768]{2,1,0:T(8,128)S(1)} %get-tuple-element.9.sg_ref, bf16[2,64,768]{2,1,0:T(8,128)(2,1)S(1)} %collective-permute-done.2.low_ref, bf16[2,64,768]{2,1,0:T(8,128)(2,1)S(1)} %collective-permute-done.3.high_ref, bf16[4,768,360]{2,1,0:T(8,128)(2,1)S(1)} %copy-done.11), custom_call_target="tpu_custom_call" | custom-call | flops 5000000000 | bytes 6000000 | tf_op jit(solution)/shard_map/pallas_call | solution.py:158
  111.8 1.2 copy-done.3
  113.0 9.5 %all-to-all-done.1 = bf16[4,4,180,256]{3,1,2,0:T(4,128)(2,1)} async-done(((bf16[4,4,180,256]{3,1,2,0:T(4,128)(2,1)}), bf16[4,4,180,256]{3,1,2,0:T(4,128)(2,1)}, u32[]{:S(2)}, u32[]{:S(2)}) %all-to-all-start.1) | async-done | bytes 1474592 | tf_op jit(solution)/shard_map/all_to_all | solution.py:326
  122.5 3.6 %all-to-all-start.2 = ((bf16[4,8,64,360]{3,2,1,0:T(8,128)(2,1)}), bf16[4,8,64,360]{3,2,1,0:T(8,128)(2,1)S(1)}, u32[]{:S(2)}, u32[]{:S(2)}) async-start(bf16[4,8,64,360]{3,2,1,0:T(8,128)(2,1)} %copy-done.3), calls=%async_computation.2 | async-start | bytes 3145728 | tf_op jit(solution)/shard_map/all_to_all | solution.py:317
  126.1 1.0 reduce_sum.25
  127.1 14.3 %all_gather.7 = bf16[576,256]{1,0:T(8,128)(2,1)S(1)} all-gather(bf16[72,256]{1,0:T(8,128)(2,1)S(1)} %reduce_sum.25), channel_id=1, replica_groups=mesh['ens'=4,'polar'=2,'azimuth'=4] {'ens','polar'}, dimensions={0}, use_global_device_ids=true | all-gather | bytes 331776 | tf_op jit(solution)/shard_map/all_gather | solution.py:328
  141.3 0.9 convert.17
  142.2 2.3 %reduce_sum.24 = bf16[4,180,256]{2,0,1:T(4,128)(2,1)S(1)} reduce(bf16[4,4,180,256]{3,1,2,0:T(4,128)(2,1)} %all-to-all-done.1, bf16[]{:T(256)} %constant.9.clone.1), dimensions={0}, to_apply=%region_0.1 | reduce | flops 552960 | bytes 1843202 | tf_op jit(solution)/shard_map/reduce_sum | solution.py:330
  144.5 0.9 copy.32
  145.4 1.4 copy.31
  146.8 2.6 %copy.33 = bf16[1,8,360,256]{3,2,1,0:T(8,128)(2,1)} copy(bf16[1,8,360,256]{2,3,1,0:T(8,128)(2,1)} %bitcast.26) | data formatting | bytes 2949120
  (33 shorter events, 0.2 us)
Async XLA Ops:
  7.2 10.8 %copy-start = (bf16[9,256,256]{2,1,0:T(8,128)(2,1)S(1)}, bf16[9,256,256]{2,1,0:T(8,128)(2,1)}, u32[]{:S(2)}) copy-start(bf16[9,256,256]{2,1,0:T(8,128)(2,1)} %param.12) | copy-start | bytes 3538948
  7.2 44.4 %all-gather.2.cloned.1.call-start = ((), (), s32[]{:S(2)}) async-start(), calls=%async_computation.4 | async-start | bytes 1843200 | tf_op jit(solution)/shard_map/all_gather | solution.py:305
  11.2 5.3 %copy-start.16 = (s32[4,2]{0,1:T(2,128)S(1)}, s32[4,2]{0,1:T(2,128)}, u32[]{:S(2)}) copy-start(s32[4,2]{0,1:T(2,128)} %param.11) | copy-start | bytes 100
  11.2 5.3 %copy-start.15 = (bf16[9,4,5,720]{3,1,2,0:T(4,128)(2,1)S(1)}, bf16[9,4,5,720]{3,1,2,0:T(4,128)(2,1)}, u32[]{:S(2)}) copy-start(bf16[9,4,5,720]{3,1,2,0:T(4,128)(2,1)} %param.10) | copy-start | bytes 777604
  11.2 28.5 %all-to-all-start = ((bf16[4,8,64,360]{3,2,1,0:T(8,128)(2,1)}), bf16[4,8,64,360]{3,2,1,0:T(8,128)(2,1)S(1)}, u32[]{:S(2)}, u32[]{:S(2)}) async-start(bf16[4,8,64,360]{3,2,1,0:T(8,128)(2,1)} %bitcast.24), calls=%async_computation | async-start | bytes 3145728 | tf_op jit(solution)/shard_map/all_to_all | solution.py:307
  18.0 25.8 %copy-start.5 = (bf16[9,64,256]{2,1,0:T(8,128)(2,1)}, bf16[9,64,256]{2,1,0:T(8,128)(2,1)S(1)}, u32[]{:S(2)}) copy-start(bf16[9,64,256]{2,1,0:T(8,128)(2,1)S(1)} %constant_dynamic-slice_fusion.refs_2_) | copy-start | bytes 884740
  39.7 1.6 %copy-start.12 = (bf16[4,360,768]{2,1,0:T(8,128)(2,1)S(1)}, bf16[4,360,768]{2,1,0:T(8,128)(2,1)}, u32[]{:S(2)}) copy-start(bf16[4,360,768]{2,1,0:T(8,128)(2,1)} %constant.27.clone.table_ref) | copy-start | bytes 6635524
  43.8 1.3 copy-start.1
  45.1 26.3 %collective-permute-start = (bf16[2,64,768]{2,1,0:T(8,128)(2,1)}, bf16[2,64,768]{2,1,0:T(8,128)(2,1)}, u32[]{:S(2)}, u32[]{:S(2)}) collective-permute-start(bf16[2,64,768]{2,1,0:T(8,128)(2,1)} %get-tuple-element.20), channel_id=1, source_target_pairs={{0,4},{1,5},{2,6},{3,7},{8,12},{9,13},{10,14},{11,15},{16,20},{17,... | collective-permute-start | bytes 589832 | tf_op jit(solution)/shard_map/ppermute | solution.py:292
  47.1 24.3 %collective-permute-start.1 = (bf16[2,64,768]{2,1,0:T(8,128)(2,1)}, bf16[2,64,768]{2,1,0:T(8,128)(2,1)}, u32[]{:S(2)}, u32[]{:S(2)}) collective-permute-start(bf16[2,64,768]{2,1,0:T(8,128)(2,1)} %get-tuple-element.19), channel_id=1, source_target_pairs={{4,0},{5,1},{6,2},{7,3},{12,8},{13,9},{14,10},{15,11},{20,16},{21,... | collective-permute-start | bytes 589832 | tf_op jit(solution)/shard_map/ppermute | solution.py:292
  53.1 1.0 copy-start.6
  54.1 1.2 copy-start.7
  55.2 1.4 copy-start.13
  56.7 14.7 %copy-start.2 = (f32[8,64,768]{2,1,0:T(8,128)S(1)}, f32[8,64,768]{2,1,0:T(8,128)}, u32[]{:S(2)}) copy-start(f32[8,64,768]{2,1,0:T(8,128)} %copy-done.1) | copy-start | bytes 4718596
  56.7 14.7 %copy-start.8 = (f32[4,9,16,384]{3,2,1,0:T(8,128)S(1)}, f32[4,9,16,384]{3,2,1,0:T(8,128)}, u32[]{:S(2)}) copy-start(f32[4,9,16,384]{3,2,1,0:T(8,128)} %pad_convert_fusion.refs_3_) | copy-start | bytes 2654212
  56.7 14.7 %copy-start.9 = (bf16[576,256]{0,1:T(8,128)(2,1)S(1)}, bf16[576,256]{0,1:T(8,128)(2,1)}, u32[]{:S(2)}) copy-start(bf16[576,256]{0,1:T(8,128)(2,1)} %copy.28) | copy-start | bytes 884740
  56.7 14.8 %copy-start.14 = (bf16[4,180,768]{2,1,0:T(8,128)(2,1)S(1)}, bf16[4,180,768]{2,1,0:T(8,128)(2,1)}, u32[]{:S(2)}) copy-start(bf16[4,180,768]{2,1,0:T(8,128)(2,1)} %constant.28.clone.refs_6_) | copy-start | bytes 3317764
  83.0 1.2 copy-start.4
  84.1 0.7 copy-start.10
  84.9 15.2 %all-to-all-start.3 = ((bf16[8,72,256]{2,1,0:T(8,128)(2,1)}), bf16[8,72,256]{2,1,0:T(8,128)(2,1)}, u32[]{:S(2)}, u32[]{:S(2)}) async-start(bf16[8,72,256]{2,1,0:T(8,128)(2,1)} %bitcast.23), calls=%async_computation.3 | async-start | bytes 589824 | tf_op jit(solution)/shard_map/all_to_all | solution.py:325
  100.0 22.5 %all-to-all-start.1 = ((bf16[4,4,180,256]{3,1,2,0:T(4,128)(2,1)}), bf16[4,4,180,256]{3,1,2,0:T(4,128)(2,1)}, u32[]{:S(2)}, u32[]{:S(2)}) async-start(bf16[4,4,180,256]{3,1,2,0:T(4,128)(2,1)} %copy.29), calls=%async_computation.1 | async-start | bytes 2949120 | tf_op jit(solution)/shard_map/all_to_all | solution.py:326
  104.4 5.0 %copy-start.11 = (bf16[4,768,360]{2,1,0:T(8,128)(2,1)S(1)}, bf16[4,768,360]{2,1,0:T(8,128)(2,1)}, u32[]{:S(2)}) copy-start(bf16[4,768,360]{2,1,0:T(8,128)(2,1)} %constant.26.clone.table_ref) | copy-start | bytes 6635524
  104.6 2.8 %collective-permute-start.2 = (bf16[2,64,768]{2,1,0:T(8,128)(2,1)S(1)}, bf16[2,64,768]{2,1,0:T(8,128)(2,1)S(1)}, u32[]{:S(2)}, u32[]{:S(2)}) collective-permute-start(bf16[2,64,768]{2,1,0:T(8,128)(2,1)S(1)} %get-tuple-element.18), channel_id=1, source_target_pairs={{0,4},{1,5},{2,6},{3,7},{8,12},{9,13},{10,14},{11,15},{16,20},{17,... | collective-permute-start | bytes 589832 | tf_op jit(solution)/shard_map/ppermute | solution.py:292
  106.0 3.3 %collective-permute-start.3 = (bf16[2,64,768]{2,1,0:T(8,128)(2,1)S(1)}, bf16[2,64,768]{2,1,0:T(8,128)(2,1)S(1)}, u32[]{:S(2)}, u32[]{:S(2)}) collective-permute-start(bf16[2,64,768]{2,1,0:T(8,128)(2,1)S(1)} %get-tuple-element.17), channel_id=1, source_target_pairs={{4,0},{5,1},{6,2},{7,3},{12,8},{13,9},{14,10},{15,11},{20,16},{21,... | collective-permute-start | bytes 589832 | tf_op jit(solution)/shard_map/ppermute | solution.py:292
  111.8 1.2 copy-start.3
  122.5 22.9 %all-to-all-start.2 = ((bf16[4,8,64,360]{3,2,1,0:T(8,128)(2,1)}), bf16[4,8,64,360]{3,2,1,0:T(8,128)(2,1)S(1)}, u32[]{:S(2)}, u32[]{:S(2)}) async-start(bf16[4,8,64,360]{3,2,1,0:T(8,128)(2,1)} %copy-done.3), calls=%async_computation.2 | async-start | bytes 3145728 | tf_op jit(solution)/shard_map/all_to_all | solution.py:317
Sparse Core Ops, SparseCore 0:
  9.9 41.6 all-gather.1
where the time goes:
time: 157 us; the launch traced here: 156 us
  waiting for transfers between devices  41.7 us (27%)
  Pallas kernels  31.1 us (20%)
  local copies, waits for them, and re-layouts  24.4 us (16%)
  starting transfers between devices  23.9 us (15%)
  blocking collectives  14.3 us (9%)
  between operations  14.3 us (9%)
  other arithmetic  6.55 us (4%)
    all_to_all x1, waiting for transfers between devices, local(): spread = lax.all_to_all(pieces, 'azimuth', 0, 0)  18.8 us
    pallas_call x1, Pallas kernels, backward_spectra(): pl.pallas_call(lambda *refs: back_kernel(window, *refs), grid=(outs,), in...  14.7 us
    all_gather x1, blocking collectives, local(): weight_grad = lax.all_gather(summed, axes, axis=0, tiled=True)  14.3 us
    unnamed x38, local copies, waits for them, and re-layouts  13.9 us
    pallas_call x1, Pallas kernels, mix(): pl.pallas_call(lambda *refs: mix_kernel(window, *refs), grid=(outs,), in_...  11.6 us
    all_to_all x1, waiting for transfers between devices, local(): conv_terms = lax.all_to_all(conv_parts, 'azimuth', 0, 0)  9.49 us
    all_to_all x1, waiting for transfers between devices, local(): terms = lax.all_to_all(wg.reshape(count, -1, d), axes, 0, 0)  7.49 us
    ppermute x4, starting transfers between devices, to_neighbours(): return (lax.ppermute(last, 'polar', up), lax.ppermute(first, 'polar', down))  6 us
  transfers between devices with their start and end apart: 9, of which 5 were waited for; matrix products, arithmetic and copies ran while one was open for 12% of the time, Pallas kernels for 13%

commit v1 on v0

--- a/solution.py
+++ b/solution.py
@@ -41,7 +41,7 @@
         forward,
         np.ascontiguousarray(forward.transpose(0, 2, 1)),
         np.ascontiguousarray(inverse.transpose(1, 0, 2)),
-        np.ascontiguousarray(inverse.transpose(1, 2, 0)),
+        np.pad(inverse.transpose(1, 2, 0), ((0, 0), (0, -inverse.shape[2] % ROWS), (0, 0))),
     )
 
 
@@ -200,16 +200,88 @@
 
 
 def mix_kernel(window, x_ref, low_ref, high_ref, mk_ref, gs_ref, wt_ref, inv_ref,
-               conv_ref, wg_ref, ext_ref, mixed_ref, total_ref):
+               conv_ref, wg_ref, ext_ref, mixed_ref, total_ref,
+               conv_send, conv_recv, piece_send, piece_recv, sums,
+               conv_out_sem, conv_in_sem, piece_out_sem, piece_in_sem, sum_out_sem, sum_in_sem):
     o = pl.program_id(0)
     rows, share, columns = x_ref.shape
     rim = low_ref.shape[0]
     taps = mixed_ref.shape[0]
     wide = columns // 2
     block = min(ROWS, share)
+    shares, outs = conv_send.shape[:2]
+    count, piece = piece_send.shape[:2]
+    part = conv_ref.shape[1]
+    me = lax.axis_index("azimuth")
+    bands = lax.axis_size("polar")
+    rank = lax.axis_index("ens") * bands + lax.axis_index("polar")
+
+    def across(step):
+        other = lax.rem(me + step, shares)
+        return other, {"azimuth": other}
+
+    def along(step):
+        other = lax.rem(rank + step, count)
+        return other, {"ens": lax.div(other, bands), "polar": lax.rem(other, bands)}
+
+    def conv_copy(row, step):
+        other, device = across(step)
+        return pltpu.make_async_remote_copy(
+            src_ref=conv_send.at[other, row],
+            dst_ref=conv_recv.at[me, row],
+            send_sem=conv_out_sem.at[step, row],
+            recv_sem=conv_in_sem.at[me, row],
+            device_id=device,
+            device_id_type=pl.DeviceIdType.MESH,
+        )
+
+    def conv_arrival(row, step):
+        other, device = across(step)
+        return pltpu.make_async_remote_copy(
+            src_ref=conv_send.at[other, row],
+            dst_ref=conv_recv.at[other, row],
+            send_sem=conv_out_sem.at[step, row],
+            recv_sem=conv_in_sem.at[other, row],
+            device_id=device,
+            device_id_type=pl.DeviceIdType.MESH,
+        )
+
+    def piece_copy(step, landing):
+        other, device = along(step)
+        at = rank if landing is None else other
+        return pltpu.make_async_remote_copy(
+            src_ref=piece_send.at[other],
+            dst_ref=piece_recv.at[at],
+            send_sem=piece_out_sem.at[step],
+            recv_sem=piece_in_sem.at[at],
+            device_id=device,
+            device_id_type=pl.DeviceIdType.MESH,
+        )
+
+    def sum_copy(step, landing):
+        other, device = along(step)
+        at = rank if landing is None else other
+        return pltpu.make_async_remote_copy(
+            src_ref=sums.at[at],
+            dst_ref=sums.at[at],
+            send_sem=sum_out_sem.at[step],
+            recv_sem=sum_in_sem.at[at],
+            device_id=device,
+            device_id_type=pl.DeviceIdType.MESH,
+        )
 
     @pl.when(o == 0)
     def _():
+        barrier = pltpu.get_barrier_semaphore()
+        for step in range(1, shares):
+            pl.semaphore_signal(
+                barrier, inc=1, device_id=across(step)[1], device_id_type=pl.DeviceIdType.MESH
+            )
+        for step in range(1, count):
+            pl.semaphore_signal(
+                barrier, inc=1, device_id=along(step)[1], device_id_type=pl.DeviceIdType.MESH
+            )
+        pl.semaphore_wait(barrier, shares + count - 2)
         ext_ref[0:rim] = low_ref[...].astype(F32)
         ext_ref[rim : rim + rows] = x_ref[...]
         ext_ref[rim + rows :] = high_ref[...].astype(F32)
@@ -237,24 +309,64 @@
                 mixed_ref[k, here, im] = mi.astype(BF16)
 
     mixed = mixed_ref[...].reshape(taps * share, columns)
-    total_ref[...] += jnp.dot(mixed, gs_ref[0], preferred_element_type=F32)
+    total_ref[0 : taps * share] += jnp.dot(mixed, gs_ref[0], preferred_element_type=F32)
+
+    @pl.when(o == outs - 1)
+    def _():
+        for p in range(count):
+            piece_send[p] = total_ref[p * piece : (p + 1) * piece].astype(BF16)
+        for step in range(1, count):
+            piece_copy(step, None).start()
+        piece_recv[rank] = piece_send[rank]
+
     spec = jnp.dot(wt_ref[...], mixed, preferred_element_type=F32).astype(BF16)
-    for s in range(inv_ref.shape[0]):
-        conv_ref[s, 0] = lax.dot_general(
-            inv_ref[s], spec, NT, preferred_element_type=F32
-        ).astype(BF16)
-
-    @pl.when(o == pl.num_programs(0) - 1)
+    for step in list(range(1, shares)) + [0]:
+        other = across(step)[0]
+        term = lax.dot_general(inv_ref[other], spec, NT, preferred_element_type=F32).astype(BF16)
+        if step == 0:
+            conv_recv[me, o] = term
+        else:
+            conv_send[other, o] = term
+            conv_copy(o, step).start()
+
+    @pl.when(o == outs - 1)
     def _():
-        wg_ref[...] = total_ref[...].astype(BF16)
-
-
-def mix(x, low, high, filters, gs, weights_t, inverse_t, window):
+        for step in range(1, count):
+            piece_copy(step, True).wait_recv()
+        whole_sum = piece_recv[0].astype(F32)
+        for p in range(1, count):
+            whole_sum += piece_recv[p].astype(F32)
+        sums[rank] = whole_sum.astype(BF16)
+        for step in range(1, count):
+            sum_copy(step, None).start()
+        for row in range(outs):
+            for step in range(1, shares):
+                conv_arrival(row, step).wait_recv()
+        for row in range(outs):
+            result = conv_recv[0, row].astype(F32)
+            for s in range(1, shares):
+                result += conv_recv[s, row].astype(F32)
+            conv_ref[row] = result.astype(BF16)[:part]
+        for step in range(1, count):
+            sum_copy(step, True).wait_recv()
+        wg_ref[...] = sums[...].astype(F32).reshape(count * piece, -1)[: taps * share]
+        for row in range(outs):
+            for step in range(1, shares):
+                conv_copy(row, step).wait_send()
+        for step in range(1, count):
+            piece_copy(step, None).wait_send()
+            sum_copy(step, None).wait_send()
+
+
+def mix(x, low, high, filters, gs, weights_t, inverse_t, window, part):
     rows, share, columns = x.shape
     rim = low.shape[0]
     outs, taps = filters.shape[:2]
     d = gs.shape[2]
-    shares, part, _ = inverse_t.shape
+    shares, padded, _ = inverse_t.shape
+    count = lax.axis_size("ens") * lax.axis_size("polar")
+    piece = -(-taps * share // (count * ROWS)) * ROWS
+    dma = pltpu.SemaphoreType.DMA
     return pl.pallas_call(
         lambda *refs: mix_kernel(window, *refs),
         grid=(outs,),
@@ -267,20 +379,33 @@
             whole(weights_t.shape),
             whole(inverse_t.shape),
         ],
-        out_specs=[
-            pl.BlockSpec((shares, 1, part, d), lambda i: (0, i, 0, 0)),
-            whole((taps * share, d)),
-        ],
+        out_specs=[whole((outs, part, d)), whole((taps * share, d))],
         out_shape=[
-            jax.ShapeDtypeStruct((shares, outs, part, d), BF16),
-            jax.ShapeDtypeStruct((taps * share, d), BF16),
+            jax.ShapeDtypeStruct((outs, part, d), BF16),
+            jax.ShapeDtypeStruct((taps * share, d), F32),
         ],
         scratch_shapes=[
             pltpu.VMEM((rows + 2 * rim, share, columns), F32),
             pltpu.VMEM((taps, share, columns), BF16),
-            pltpu.VMEM((taps * share, d), F32),
-        ],
-        compiler_params=params(),
+            pltpu.VMEM((count * piece, d), F32),
+            pltpu.VMEM((shares, outs, padded, d), BF16),
+            pltpu.VMEM((shares, outs, padded, d), BF16),
+            pltpu.VMEM((count, piece, d), BF16),
+            pltpu.VMEM((count, piece, d), BF16),
+            pltpu.VMEM((count, piece, d), BF16),
+            dma((shares, outs)),
+            dma((shares, outs)),
+            dma((count,)),
+            dma((count,)),
+            dma((count,)),
+            dma((count,)),
+        ],
+        compiler_params=pltpu.CompilerParams(
+            dimension_semantics=("arbitrary",),
+            vmem_limit_bytes=40 * 1024 * 1024,
+            collective_id=0,
+            has_side_effects=True,
+        ),
         cost_estimate=cost(2e10, 1e7),
     )(x, low, high, filters, gs, weights_t, inverse_t)
 
@@ -316,18 +441,13 @@
     grad_pieces = field_gradient(sg, low, high, jnp.asarray(forward_t))
     grad_back = lax.all_to_all(grad_pieces, "azimuth", 0, 0)
 
+    spread, _ = lax.optimization_barrier((spread, grad_pieces))
     x = input_spectra(spread, jnp.asarray(forward), margin)
     low, high = to_neighbours(x[:margin].astype(BF16), x[rows - margin :].astype(BF16))
-    conv_parts, wg = mix(x, low, high, filters, gs, own_t, jnp.asarray(inverse_t), window)
-
-    axes = ("ens", "polar")
-    count = lax.axis_size("ens") * lax.axis_size("polar")
-    terms = lax.all_to_all(wg.reshape(count, -1, d), axes, 0, 0)
-    conv_terms = lax.all_to_all(conv_parts, "azimuth", 0, 0)
-    summed = jnp.sum(terms.astype(F32), axis=0).astype(BF16)
-    weight_grad = lax.all_gather(summed, axes, axis=0, tiled=True)
-    weight_grad = weight_grad.reshape(taps, share, d).astype(F32)
-    conv_out = jnp.sum(conv_terms.astype(F32), axis=0).astype(BF16)
+    conv_out, weight_grad = mix(
+        x, low, high, filters, gs, own_t, jnp.asarray(inverse_t), window, out_grad.shape[2]
+    )
+    weight_grad = weight_grad.reshape(taps, share, d)
     field_grad = grad_back.transpose(1, 3, 0, 2).reshape(rows, part, channels)
     return (conv_out[None], field_grad[None], weight_grad)
 

time: 157 us -> 144 us (0.917)
  Pallas kernels: 31.1 us -> 52.8 us
  blocking collectives: 14.3 us -> 0 us
  starting transfers between devices: 23.9 us -> 16.3 us
  waiting for transfers between devices: 41.7 us -> 34.3 us
  other arithmetic: 6.55 us -> 2.42 us
  local copies, waits for them, and re-layouts: 24.4 us -> 22.6 us
    all_gather x1, waiting for transfers between devices: 3.19 us -> 31.5 us  [local(): gathered = lax.all_gather(out_grad[0], 'azimuth', axis=0)]
    pallas_call x1, Pallas kernels: 11.6 us -> 32.5 us  [mix(): pl.pallas_call(lambda *refs: mix_kernel(window, *refs), grid=(outs,), in_...]
    all_to_all x1, waiting for transfers between devices: 18.8 us -> 0.01 us  [local(): spread = lax.all_to_all(pieces, 'azimuth', 0, 0)]
    all_to_all x2 -> x0, waiting for transfers between devices: 17 us -> none  [the longest x1 9.49 us: local(): conv_terms = lax.all_to_all(conv_parts, 'azimuth', 0, 0)]
    all_gather x1 -> x0, blocking collectives: 14.3 us -> none  [local(): weight_grad = lax.all_gather(summed, axes, axis=0, tiled=True)]
    all_to_all x2 -> x0, starting transfers between devices: 8.96 us -> none  [the longest x1 4.61 us: local(): terms = lax.all_to_all(wg.reshape(count, -1, d), axes, 0, 0)]
    reduce_sum x2 -> x0, other arithmetic: 3.26 us -> none  [the longest x1 2.25 us: local(): conv_out = jnp.sum(conv_terms.astype(F32), axis=0).astype(BF16)]
    pallas_call x1 -> x0, local copies, waits for them, and re-layouts: 3.06 us -> none  [mix(): pl.pallas_call(lambda *refs: mix_kernel(window, *refs), grid=(outs,), in_...]
  transfers between devices with their start and end apart: 9 -> 7, of which waited for: 5 -> 2; matrix products, arithmetic and copies ran while one was open for 12% -> 7% of each run, Pallas kernels for 13% -> 35%
where the time goes in v1:
time: 144 us; the launch traced here: 143 us
  Pallas kernels  52.8 us (37%)
  waiting for transfers between devices  34.3 us (24%)
  local copies, waits for them, and re-layouts  22.6 us (16%)
  starting transfers between devices  16.3 us (11%)
  between operations  14.3 us (10%)
  other arithmetic  2.42 us (2%)
    pallas_call x1, Pallas kernels, mix(): pl.pallas_call(lambda *refs: mix_kernel(window, *refs), grid=(outs,), in_...  32.5 us
    all_gather x1, waiting for transfers between devices, local(): gathered = lax.all_gather(out_grad[0], 'azimuth', axis=0)  31.5 us
    unnamed x36, local copies, waits for them, and re-layouts  15.7 us
    pallas_call x1, Pallas kernels, backward_spectra(): pl.pallas_call(lambda *refs: back_kernel(window, *refs), grid=(outs,), in...  14.7 us
    ppermute x4, starting transfers between devices, to_neighbours(): return (lax.ppermute(last, 'polar', up), lax.ppermute(first, 'polar', down))  6.51 us
    all_to_all x1, starting transfers between devices, local(): spread = lax.all_to_all(pieces, 'azimuth', 0, 0)  5.29 us
    all_to_all x1, starting transfers between devices, local(): grad_back = lax.all_to_all(grad_pieces, 'azimuth', 0, 0)  4.47 us
    pallas_call x1, Pallas kernels, field_gradient(): pl.pallas_call(field_grad_kernel, grid=(rows // rim,), in_specs=[pl.Block...  3.23 us
  transfers between devices with their start and end apart: 7, of which 2 were waited for; matrix products, arithmetic and copies ran while one was open for 7% of the time, Pallas kernels for 35%

profile of v1, /device:TPU:0, one launch (start us, length us, event | category | flops | bytes accessed | tf_op | source)
XLA Modules:
  0.0 142.7 jit_solution(557878313752037297)
XLA Ops:
  7.2 0.0 copy-start
  7.2 0.0 all-gather.2.cloned.1.call-start
  7.2 0.7 all-gather.2.cloned.1.call-update
  7.9 1.9 %copy.25 = bf16[1,8,360,256]{2,3,1,0:T(8,128)(2,1)S(1)} copy(bf16[1,8,360,256]{3,2,1,0:T(8,128)(2,1)} %param.9) | data formatting | bytes 2949120 | tf_op args[0]
  9.8 1.4 copy.37
  11.2 5.3 %all-to-all-start = ((bf16[4,8,64,360]{3,2,1,0:T(8,128)(2,1)}), bf16[4,8,64,360]{3,2,1,0:T(8,128)(2,1)S(1)}, u32[]{:S(2)}, u32[]{:S(2)}) async-start(bf16[4,8,64,360]{3,2,1,0:T(8,128)(2,1)} %bitcast.21), calls=%async_computation | async-start | bytes 3145728 | tf_op jit(solution)/shard_map/all_to_all | solution.py:432
  16.5 0.0 copy-done.15
  16.5 0.2 broadcast_select_fusion
  16.7 1.2 reshape.66
  18.0 2.0 %pad_convert_fusion.refs_3_ = f32[4,9,16,384]{3,2,1,0:T(8,128)} fusion(bf16[4,9,10,360]{3,2,1,0:T(8,128)(2,1)} %bitcast.24), kind=kLoop, calls=%fused_computation.1 | loop fusion | flops 221184 | bytes 1143936 | tf_op jit(solution)/shard_map/jit(_pad)/pad | solution.py:56
  20.0 31.5 %all-gather.2.cloned.1.call-done = bf16[4,4,180,256]{3,1,2,0:T(4,128)(2,1)} async-done(((bf16[1,4,180,256]{3,1,2,0:T(4,128)(2,1)}), bf16[4,4,180,256]{3,1,2,0:T(4,128)(2,1)}) %all-gather.2.cloned.1.call-update) | async-done | bytes 1474576 | tf_op jit(solution)/shard_map/all_gather | solution.py:430
  51.5 1.7 %copy.29.refs_0_ = bf16[4,4,180,256]{3,2,1,0:T(8,128)(2,1)S(1)} copy(bf16[4,4,180,256]{3,1,2,0:T(4,128)(2,1)} %all-gather.2.cloned.1.call-done) | data formatting | bytes 2949120 | tf_op jit(solution)/shard_map/all_gather | solution.py:430
  53.3 0.0 copy-done.3
  53.3 0.4 copy-done.10
  53.6 14.7 %shard_map.112 = (bf16[4,768,256]{2,1,0:T(8,128)(2,1)S(1)}, f32[12,64,768]{2,1,0:T(8,128)S(1)}) custom-call(bf16[4,4,180,256]{3,2,1,0:T(8,128)(2,1)S(1)} %copy.29.refs_0_, bf16[4,768,180]{2,1,0:T(8,128)(2,1)S(1)} %copy-done.10, bf16[9,64,256]{2,1,0:T(8,128)(2,1)S(1)} %constant_dynamic-slice_fusion.refs_2_, f32[4,9,16,384]{3,2,1,0:T(8,128)S(1)} %copy-done.3), custom_call_target="tpu_custom_call" | custom-call | flops 20000000000 | bytes 10000000 | tf_op jit(solution)/shard_map/pallas_call | solution.py:119
  68.3 0.0 copy-start.12
  68.3 0.0 copy-start.8
  68.3 0.1 convert.12
  68.5 1.0 copy-done.12
  69.6 1.9 %collective-permute-start = (bf16[2,64,768]{2,1,0:T(8,128)(2,1)S(1)}, bf16[2,64,768]{2,1,0:T(8,128)(2,1)S(1)}, u32[]{:S(2)}, u32[]{:S(2)}) collective-permute-start(bf16[2,64,768]{2,1,0:T(8,128)(2,1)S(1)} %get-tuple-element.23), channel_id=1, source_target_pairs={{0,4},{1,5},{2,6},{3,7},{8,12},{9,13},{10,14},{11,15},{16,20},{17,... | collective-permute-start | bytes 589832 | tf_op jit(solution)/shard_map/ppermute | solution.py:417
  71.4 1.3 collective-permute-start.1
  72.7 0.0 collective-permute-done.low_ref
  72.8 2.0 %collective-permute-done.1.high_ref = bf16[2,64,768]{2,1,0:T(8,128)(2,1)S(1)} collective-permute-done((bf16[2,64,768]{2,1,0:T(8,128)(2,1)S(1)}, bf16[2,64,768]{2,1,0:T(8,128)(2,1)S(1)}, u32[]{:S(2)}, u32[]{:S(2)}) %collective-permute-start.1) | collective-permute-done | bytes 196640 | tf_op jit(solution)/shard_map/ppermute | solution.py:417
  74.8 3.2 %shard_map.113 = bf16[4,8,64,360]{3,2,1,0:T(8,128)(2,1)} custom-call(f32[12,64,768]{2,1,0:T(8,128)S(1)} %get-tuple-element.8.sg_ref, bf16[2,64,768]{2,1,0:T(8,128)(2,1)S(1)} %collective-permute-done.low_ref, bf16[2,64,768]{2,1,0:T(8,128)(2,1)S(1)} %collective-permute-done.1.high_ref, bf16[4,768,360]{2,1,0:T(8,128)(2,1)S(1)} %copy-done.8), custom_call_target="tpu_custom_call" | custom-call | flops 5000000000 | bytes 6000000 | tf_op jit(solution)/shard_map/pallas_call | solution.py:158
  78.0 0.0 all-to-all-done.x_ref
  78.0 1.6 %copy-done.9 = bf16[4,360,768]{2,1,0:T(8,128)(2,1)S(1)} copy-done((bf16[4,360,768]{2,1,0:T(8,128)(2,1)S(1)}, bf16[4,360,768]{2,1,0:T(8,128)(2,1)}, u32[]{:S(2)}) %copy-start.9) | copy-done | bytes 2211864
  79.6 2.4 %shard_map.114.refs_0_ = f32[8,64,768]{2,1,0:T(8,128)S(1)} custom-call(bf16[4,8,64,360]{3,2,1,0:T(8,128)(2,1)S(1)} %all-to-all-done.x_ref, bf16[4,360,768]{2,1,0:T(8,128)(2,1)S(1)} %copy-done.9), custom_call_target="tpu_custom_call" | custom-call | flops 5000000000 | bytes 6000000 | tf_op jit(solution)/shard_map/pallas_call | solution.py:188
  82.1 0.1 convert.13
  82.2 1.1 copy-done.1
  83.3 2.0 %collective-permute-start.2 = (bf16[2,64,768]{2,1,0:T(8,128)(2,1)S(1)}, bf16[2,64,768]{2,1,0:T(8,128)(2,1)S(1)}, u32[]{:S(2)}, u32[]{:S(2)}) collective-permute-start(bf16[2,64,768]{2,1,0:T(8,128)(2,1)S(1)} %get-tuple-element.25), channel_id=1, source_target_pairs={{0,4},{1,5},{2,6},{3,7},{8,12},{9,13},{10,14},{11,15},{16,20},{17,... | collective-permute-start | bytes 589832 | tf_op jit(solution)/shard_map/ppermute | solution.py:417
  85.3 1.3 collective-permute-start.3
  86.6 0.9 copy.30
  87.5 4.5 %all-to-all-start.1 = ((bf16[4,8,64,360]{3,2,1,0:T(8,128)(2,1)}), bf16[4,8,64,360]{3,2,1,0:T(8,128)(2,1)}, u32[]{:S(2)}, u32[]{:S(2)}) async-start(bf16[4,8,64,360]{3,2,1,0:T(8,128)(2,1)} %shard_map.113), calls=%async_computation.1 | async-start | bytes 3145728 | tf_op jit(solution)/shard_map/all_to_all | solution.py:442
  92.0 0.0 collective-permute-done.2.refs_1_
  92.0 0.0 collective-permute-done.3.refs_2_
  92.0 0.0 copy-start.6
  92.1 0.7 copy-done.6
  92.7 1.2 copy-done.4
  93.9 1.0 copy-done.5
  94.9 0.9 copy-done.7
  95.8 1.3 copy-done.11
  97.1 1.4 copy-done.13
  98.5 32.5 %shard_map.115 = (bf16[4,180,256]{2,1,0:T(8,128)(2,1)S(1)}, f32[576,256]{1,0:T(8,128)S(1)}) custom-call(f32[8,64,768]{2,1,0:T(8,128)S(1)} %copy-done.2, bf16[2,64,768]{2,1,0:T(8,128)(2,1)S(1)} %collective-permute-done.2.refs_1_, bf16[2,64,768]{2,1,0:T(8,128)(2,1)S(1)} %copy-done.7, f32[4,9,16,384]{3,2,1,0:T(8,128)S(1)} %copy-done.4, ...), custom_call_target="tpu_custom_call" | custom-call | flops 20000000000 | bytes 10000000 | tf_op jit(solution)/shard_map/pallas_call | solution.py:370
  131.0 0.9 copy.32
  131.8 0.0 all-to-all-done.1
  131.9 1.6 %copy.31 = bf16[8,360,4,64]{1,3,2,0:T(8,128)(2,1)S(1)} copy(bf16[8,360,4,64]{1,3,0,2:T(8,128)(2,1)} %bitcast.8) | data formatting | bytes 2949120 | tf_op jit(solution)/shard_map/transpose | solution.py:451
  133.5 1.6 %copy.33 = bf16[1,8,360,256]{3,2,1,0:T(8,128)(2,1)} copy(bf16[1,8,360,256]{2,3,1,0:T(8,128)(2,1)S(1)} %bitcast.22) | data formatting | bytes 2949120
  135.1 0.8 copy.39
  (22 shorter events, 0.2 us)
Async XLA Ops:
  7.2 10.8 %copy-start = (bf16[9,256,256]{2,1,0:T(8,128)(2,1)S(1)}, bf16[9,256,256]{2,1,0:T(8,128)(2,1)}, u32[]{:S(2)}) copy-start(bf16[9,256,256]{2,1,0:T(8,128)(2,1)} %param.12) | copy-start | bytes 3538948
  7.2 44.3 %all-gather.2.cloned.1.call-start = ((), (), s32[]{:S(2)}) async-start(), calls=%async_computation.2 | async-start | bytes 1843200 | tf_op jit(solution)/shard_map/all_gather | solution.py:430
  11.2 5.3 %copy-start.15 = (s32[4,2]{0,1:T(2,128)S(1)}, s32[4,2]{0,1:T(2,128)}, u32[]{:S(2)}) copy-start(s32[4,2]{0,1:T(2,128)} %param.11) | copy-start | bytes 100
  11.2 5.3 %copy-start.14 = (bf16[9,4,5,720]{3,1,2,0:T(4,128)(2,1)S(1)}, bf16[9,4,5,720]{3,1,2,0:T(4,128)(2,1)}, u32[]{:S(2)}) copy-start(bf16[9,4,5,720]{3,1,2,0:T(4,128)(2,1)} %param.10) | copy-start | bytes 777604
  11.2 66.9 %all-to-all-start = ((bf16[4,8,64,360]{3,2,1,0:T(8,128)(2,1)}), bf16[4,8,64,360]{3,2,1,0:T(8,128)(2,1)S(1)}, u32[]{:S(2)}, u32[]{:S(2)}) async-start(bf16[4,8,64,360]{3,2,1,0:T(8,128)(2,1)} %bitcast.21), calls=%async_computation | async-start | bytes 3145728 | tf_op jit(solution)/shard_map/all_to_all | solution.py:432
  51.5 1.7 %copy-start.3 = (f32[4,9,16,384]{3,2,1,0:T(8,128)S(1)}, f32[4,9,16,384]{3,2,1,0:T(8,128)}, u32[]{:S(2)}) copy-start(f32[4,9,16,384]{3,2,1,0:T(8,128)} %pad_convert_fusion.refs_3_) | copy-start | bytes 2654212
  51.5 2.1 %copy-start.10 = (bf16[4,768,180]{2,1,0:T(8,128)(2,1)S(1)}, bf16[4,768,180]{2,1,0:T(8,128)(2,1)}, u32[]{:S(2)}) copy-start(bf16[4,768,180]{2,1,0:T(8,128)(2,1)} %constant.22.clone.refs_1_) | copy-start | bytes 3317764
  68.3 1.2 copy-start.12
  68.3 6.4 %copy-start.8 = (bf16[4,768,360]{2,1,0:T(8,128)(2,1)S(1)}, bf16[4,768,360]{2,1,0:T(8,128)(2,1)}, u32[]{:S(2)}) copy-start(bf16[4,768,360]{2,1,0:T(8,128)(2,1)} %constant.23.clone.table_ref) | copy-start | bytes 6635524
  69.6 3.2 %collective-permute-start = (bf16[2,64,768]{2,1,0:T(8,128)(2,1)S(1)}, bf16[2,64,768]{2,1,0:T(8,128)(2,1)S(1)}, u32[]{:S(2)}, u32[]{:S(2)}) collective-permute-start(bf16[2,64,768]{2,1,0:T(8,128)(2,1)S(1)} %get-tuple-element.23), channel_id=1, source_target_pairs={{0,4},{1,5},{2,6},{3,7},{8,12},{9,13},{10,14},{11,15},{16,20},{17,... | collective-permute-start | bytes 589832 | tf_op jit(solution)/shard_map/ppermute | solution.py:417
  71.4 3.3 %collective-permute-start.1 = (bf16[2,64,768]{2,1,0:T(8,128)(2,1)S(1)}, bf16[2,64,768]{2,1,0:T(8,128)(2,1)S(1)}, u32[]{:S(2)}, u32[]{:S(2)}) collective-permute-start(bf16[2,64,768]{2,1,0:T(8,128)(2,1)S(1)} %get-tuple-element.22), channel_id=1, source_target_pairs={{4,0},{5,1},{6,2},{7,3},{12,8},{13,9},{14,10},{15,11},{20,16},{21,... | collective-permute-start | bytes 589832 | tf_op jit(solution)/shard_map/ppermute | solution.py:417
  78.0 1.6 %copy-start.9 = (bf16[4,360,768]{2,1,0:T(8,128)(2,1)S(1)}, bf16[4,360,768]{2,1,0:T(8,128)(2,1)}, u32[]{:S(2)}) copy-start(bf16[4,360,768]{2,1,0:T(8,128)(2,1)} %constant.24.clone.table_ref) | copy-start | bytes 6635524
  82.1 1.2 copy-start.1
  83.3 8.7 %collective-permute-start.2 = (bf16[2,64,768]{2,1,0:T(8,128)(2,1)S(1)}, bf16[2,64,768]{2,1,0:T(8,128)(2,1)S(1)}, u32[]{:S(2)}, u32[]{:S(2)}) collective-permute-start(bf16[2,64,768]{2,1,0:T(8,128)(2,1)S(1)} %get-tuple-element.25), channel_id=1, source_target_pairs={{0,4},{1,5},{2,6},{3,7},{8,12},{9,13},{10,14},{11,15},{16,20},{17,... | collective-permute-start | bytes 589832 | tf_op jit(solution)/shard_map/ppermute | solution.py:417
  85.3 6.7 %collective-permute-start.3 = (bf16[2,64,768]{2,1,0:T(8,128)(2,1)S(1)}, bf16[2,64,768]{2,1,0:T(8,128)(2,1)S(1)}, u32[]{:S(2)}, u32[]{:S(2)}) collective-permute-start(bf16[2,64,768]{2,1,0:T(8,128)(2,1)S(1)} %get-tuple-element.24), channel_id=1, source_target_pairs={{4,0},{5,1},{6,2},{7,3},{12,8},{13,9},{14,10},{15,11},{20,16},{21,... | collective-permute-start | bytes 589832 | tf_op jit(solution)/shard_map/ppermute | solution.py:417
  87.5 5.2 %copy-start.2 = (f32[8,64,768]{2,1,0:T(8,128)S(1)}, f32[8,64,768]{2,1,0:T(8,128)}, u32[]{:S(2)}) copy-start(f32[8,64,768]{2,1,0:T(8,128)} %copy-done.1) | copy-start | bytes 4718596
  87.5 44.3 %all-to-all-start.1 = ((bf16[4,8,64,360]{3,2,1,0:T(8,128)(2,1)}), bf16[4,8,64,360]{3,2,1,0:T(8,128)(2,1)}, u32[]{:S(2)}, u32[]{:S(2)}) async-start(bf16[4,8,64,360]{3,2,1,0:T(8,128)(2,1)} %shard_map.113), calls=%async_computation.1 | async-start | bytes 3145728 | tf_op jit(solution)/shard_map/all_to_all | solution.py:442
  92.0 0.7 copy-start.6
  92.7 1.2 copy-start.4
  93.9 1.0 copy-start.5
  94.9 0.9 copy-start.7
  95.8 1.3 copy-start.11
  97.1 1.4 copy-start.13
Sparse Core Ops, SparseCore 0:
  9.9 41.6 all-gather.1

commit v2 on v1

--- a/solution.py
+++ b/solution.py
@@ -40,7 +40,7 @@
     return (
         forward,
         np.ascontiguousarray(forward.transpose(0, 2, 1)),
-        np.ascontiguousarray(inverse.transpose(1, 0, 2)),
+        np.pad(inverse.transpose(1, 0, 2), ((0, 0), (0, 0), (0, -inverse.shape[2] % ROWS))),
         np.pad(inverse.transpose(1, 2, 0), ((0, 0), (0, -inverse.shape[2] % ROWS), (0, 0))),
     )
 
@@ -66,14 +66,86 @@
     )
 
 
+def remote_params(identity):
+    return pltpu.CompilerParams(
+        dimension_semantics=("arbitrary",),
+        vmem_limit_bytes=40 * 1024 * 1024,
+        collective_id=identity,
+        has_side_effects=True,
+    )
+
+
 def cost(flops, moved):
     return pl.CostEstimate(flops=int(flops), bytes_accessed=int(moved), transcendentals=0)
 
 
-def back_kernel(window, og_ref, inv_ref, w_ref, mk_ref, gs_ref, sg_ref, mg_ref):
+def rim_copies(send, recv, out_sem, in_sem):
+    bands = lax.axis_size("polar")
+    band = lax.axis_index("polar")
+    return [
+        pltpu.make_async_remote_copy(
+            src_ref=send.at[side],
+            dst_ref=recv.at[1 - side],
+            send_sem=out_sem.at[side],
+            recv_sem=in_sem.at[1 - side],
+            device_id={"polar": lax.rem(band + step, bands)},
+            device_id_type=pl.DeviceIdType.MESH,
+        )
+        for side, step in ((0, bands - 1), (1, 1))
+    ]
+
+
+def rim_values(recv):
+    band = lax.axis_index("polar")
+    low = jnp.where(band > 0, recv[0].astype(F32), 0.0)
+    high = jnp.where(band < lax.axis_size("polar") - 1, recv[1].astype(F32), 0.0)
+    return low, high
+
+
+def back_kernel(window, og_ref, inv_ref, w_ref, mk_ref, gs_ref, sg_ref, low_ref, high_ref,
+                mg_ref, og_all, rim_send, rim_recv,
+                og_out_sem, og_in_sem, rim_out_sem, rim_in_sem):
     o = pl.program_id(0)
-    shares = og_ref.shape[0]
+    shares, outs = og_all.shape[:2]
     taps, share, columns = mg_ref.shape
+    rim = low_ref.shape[0]
+    me = lax.axis_index("azimuth")
+    bands = lax.axis_size("polar")
+
+    def og_copy(row, step, arriving):
+        other = lax.rem(me + step, shares)
+        at = other if arriving else me
+        return pltpu.make_async_remote_copy(
+            src_ref=og_ref.at[row],
+            dst_ref=og_all.at[at, row],
+            send_sem=og_out_sem.at[step, row],
+            recv_sem=og_in_sem.at[at, row],
+            device_id={"azimuth": other},
+            device_id_type=pl.DeviceIdType.MESH,
+        )
+
+    @pl.when(o == 0)
+    def _():
+        barrier = pltpu.get_barrier_semaphore()
+        for step in range(1, shares):
+            pl.semaphore_signal(
+                barrier,
+                inc=1,
+                device_id={"azimuth": lax.rem(me + step, shares)},
+                device_id_type=pl.DeviceIdType.MESH,
+            )
+        for step in (1, bands - 1):
+            pl.semaphore_signal(
+                barrier,
+                inc=1,
+                device_id={"polar": lax.rem(lax.axis_index("polar") + step, bands)},
+                device_id_type=pl.DeviceIdType.MESH,
+            )
+        pl.semaphore_wait(barrier, shares + 1)
+        for row in range(outs):
+            for step in range(1, shares):
+                og_copy(row, step, False).start()
+
     wide = columns // 2
     block = min(ROWS, share)
 
@@ -81,9 +153,11 @@
     def _():
         sg_ref[...] = jnp.zeros_like(sg_ref)
 
-    total = jnp.dot(inv_ref[0], og_ref[0, 0], preferred_element_type=F32)
-    for s in range(1, shares):
-        total += jnp.dot(inv_ref[s], og_ref[s, 0], preferred_element_type=F32)
+    total = jnp.dot(inv_ref[me], og_ref[o], preferred_element_type=F32)
+    for step in range(1, shares):
+        other = lax.rem(me + step, shares)
+        og_copy(o, step, True).wait_recv()
+        total += jnp.dot(inv_ref[other], og_all[other, o], preferred_element_type=F32)
     gs = total.astype(BF16)
     gs_ref[0] = gs
     for k in range(taps):
@@ -112,15 +186,35 @@
                 sg_ref[2 * o + j, rows, im] += acc[j][1]
 
 
-def backward_spectra(gathered, inverse, weights, filters, window, rows_total):
-    shares, outs, part, d = gathered.shape
+    @pl.when(o == outs - 1)
+    def _():
+        copies = rim_copies(rim_send, rim_recv, rim_out_sem, rim_in_sem)
+        rim_send[0] = sg_ref[0:rim].astype(BF16)
+        rim_send[1] = sg_ref[sg_ref.shape[0] - rim :].astype(BF16)
+        for copy in copies:
+            copy.start()
+        for copy in copies:
+            copy.wait_recv()
+        low, high = rim_values(rim_recv)
+        low_ref[...] = low.astype(BF16)
+        high_ref[...] = high.astype(BF16)
+        for copy in copies:
+            copy.wait_send()
+        for row in range(outs):
+            for step in range(1, shares):
+                og_copy(row, step, False).wait_send()
+
+
+def backward_spectra(cotangent, inverse, weights, filters, window, rows_total, rim):
+    outs, padded, d = cotangent.shape
+    shares, columns, _ = inverse.shape
     taps, share, _ = weights.shape
-    columns = inverse.shape[1]
+    dma = pltpu.SemaphoreType.DMA
     return pl.pallas_call(
         lambda *refs: back_kernel(window, *refs),
         grid=(outs,),
         in_specs=[
-            pl.BlockSpec((shares, 1, part, d), lambda i: (0, i, 0, 0)),
+            whole(cotangent.shape),
             whole(inverse.shape),
             whole(weights.shape),
             pl.BlockSpec((1,) + filters.shape[1:], lambda i: (i, 0, 0, 0)),
@@ -128,15 +222,28 @@
         out_specs=[
             pl.BlockSpec((1, columns, d), lambda i: (i, 0, 0)),
             whole((rows_total, share, columns)),
+            whole((rim, share, columns)),
+            whole((rim, share, columns)),
         ],
         out_shape=[
             jax.ShapeDtypeStruct((outs, columns, d), BF16),
             jax.ShapeDtypeStruct((rows_total, share, columns), F32),
-        ],
-        scratch_shapes=[pltpu.VMEM((taps, share, columns), F32)],
-        compiler_params=params(),
+            jax.ShapeDtypeStruct((rim, share, columns), BF16),
+            jax.ShapeDtypeStruct((rim, share, columns), BF16),
+        ],
+        scratch_shapes=[
+            pltpu.VMEM((taps, share, columns), F32),
+            pltpu.VMEM((shares, outs, padded, d), BF16),
+            pltpu.VMEM((2, rim, share, columns), BF16),
+            pltpu.VMEM((2, rim, share, columns), BF16),
+            dma((shares, outs)),
+            dma((shares, outs)),
+            dma((2,)),
+            dma((2,)),
+        ],
+        compiler_params=remote_params(1),
         cost_estimate=cost(2e10, 1e7),
-    )(gathered, inverse, weights, filters)
+    )(cotangent, inverse, weights, filters)
 
 
 def field_grad_kernel(sg_ref, low_ref, high_ref, table_ref, out_ref):
@@ -171,41 +278,14 @@
     )(sg, low, high, table)
 
 
-def spectra_kernel(x_ref, table_ref, out_ref):
-    shares, rows, share, part = x_ref.shape
-    total = None
-    for s in range(shares):
-        term = jnp.dot(
-            x_ref[s].reshape(rows * share, part), table_ref[s], preferred_element_type=F32
-        )
-        total = term if total is None else total + term
-    out_ref[...] = total.reshape(out_ref.shape)
-
-
-def input_spectra(x, table, rim):
-    shares, rows, share, part = x.shape
-    columns = table.shape[2]
-    return pl.pallas_call(
-        spectra_kernel,
-        grid=(rows // rim,),
-        in_specs=[
-            pl.BlockSpec((shares, rim, share, part), lambda i: (0, i, 0, 0)),
-            whole(table.shape),
-        ],
-        out_specs=pl.BlockSpec((rim, share, columns), lambda i: (i, 0, 0)),
-        out_shape=jax.ShapeDtypeStruct((rows, share, columns), F32),
-        compiler_params=params(),
-        cost_estimate=cost(5e9, 6e6),
-    )(x, table)
-
-
-def mix_kernel(window, x_ref, low_ref, high_ref, mk_ref, gs_ref, wt_ref, inv_ref,
+def mix_kernel(window, x_ref, table_ref, mk_ref, gs_ref, wt_ref, inv_ref,
                conv_ref, wg_ref, ext_ref, mixed_ref, total_ref,
-               conv_send, conv_recv, piece_send, piece_recv, sums,
-               conv_out_sem, conv_in_sem, piece_out_sem, piece_in_sem, sum_out_sem, sum_in_sem):
+               conv_send, conv_recv, piece_send, piece_recv, sums, rim_send, rim_recv,
+               rim_out_sem, rim_in_sem, conv_out_sem, conv_in_sem, piece_out_sem, piece_in_sem, sum_out_sem, sum_in_sem):
     o = pl.program_id(0)
-    rows, share, columns = x_ref.shape
-    rim = low_ref.shape[0]
+    _, rows, share, length = x_ref.shape
+    columns = table_ref.shape[2]
+    rim = rim_send.shape[1]
     taps = mixed_ref.shape[0]
     wide = columns // 2
     block = min(ROWS, share)
@@ -282,9 +362,31 @@
                 barrier, inc=1, device_id=along(step)[1], device_id_type=pl.DeviceIdType.MESH
             )
         pl.semaphore_wait(barrier, shares + count - 2)
-        ext_ref[0:rim] = low_ref[...].astype(F32)
-        ext_ref[rim : rim + rows] = x_ref[...]
-        ext_ref[rim + rows :] = high_ref[...].astype(F32)
+
+        def spectra(first):
+            value = None
+            for s in range(shares):
+                field = x_ref[s, first : first + rim].reshape(rim * share, length)
+                term = jnp.dot(field, table_ref[s], preferred_element_type=F32)
+                value = term if value is None else value + term
+            value = value.reshape(rim, share, columns)
+            ext_ref[rim + first : 2 * rim + first] = value
+            return value
+
+        copies = rim_copies(rim_send, rim_recv, rim_out_sem, rim_in_sem)
+        rim_send[0] = spectra(0).astype(BF16)
+        copies[0].start()
+        rim_send[1] = spectra(rows - rim).astype(BF16)
+        copies[1].start()
+        for first in range(rim, rows - rim, rim):
+            spectra(first)
+        for copy in copies:
+            copy.wait_recv()
+        low, high = rim_values(rim_recv)
+        ext_ref[0:rim] = low
+        ext_ref[rim + rows :] = high
+        for copy in copies:
+            copy.wait_send()
         total_ref[...] = jnp.zeros_like(total_ref)
 
     for at in range(0, wide, LANES):
@@ -358,9 +460,10 @@
             sum_copy(step, None).wait_send()
 
 
-def mix(x, low, high, filters, gs, weights_t, inverse_t, window, part):
-    rows, share, columns = x.shape
-    rim = low.shape[0]
+def mix(x, table, filters, gs, weights_t, inverse_t, window, part):
+    _, rows, share, _ = x.shape
+    columns = table.shape[2]
+    rim = window // 2
     outs, taps = filters.shape[:2]
     d = gs.shape[2]
     shares, padded, _ = inverse_t.shape
@@ -372,8 +475,7 @@
         grid=(outs,),
         in_specs=[
             whole(x.shape),
-            whole(low.shape),
-            whole(high.shape),
+            whole(table.shape),
             pl.BlockSpec((1,) + filters.shape[1:], lambda i: (i, 0, 0, 0)),
             pl.BlockSpec((1, columns, d), lambda i: (i, 0, 0)),
             whole(weights_t.shape),
@@ -393,6 +495,10 @@
             pltpu.VMEM((count, piece, d), BF16),
             pltpu.VMEM((count, piece, d), BF16),
             pltpu.VMEM((count, piece, d), BF16),
+            pltpu.VMEM((2, rim, share, columns), BF16),
+            pltpu.VMEM((2, rim, share, columns), BF16),
+            dma((2,)),
+            dma((2,)),
             dma((shares, outs)),
             dma((shares, outs)),
             dma((count,)),
@@ -400,21 +506,9 @@
             dma((count,)),
             dma((count,)),
         ],
-        compiler_params=pltpu.CompilerParams(
-            dimension_semantics=("arbitrary",),
-            vmem_limit_bytes=40 * 1024 * 1024,
-            collective_id=0,
-            has_side_effects=True,
-        ),
+        compiler_params=remote_params(0),
         cost_estimate=cost(2e10, 1e7),
-    )(x, low, high, filters, gs, weights_t, inverse_t)
-
-
-def to_neighbours(first, last):
-    count = lax.axis_size("polar")
-    up = [(i, i + 1) for i in range(count - 1)]
-    down = [(i + 1, i) for i in range(count - 1)]
-    return lax.ppermute(last, "polar", up), lax.ppermute(first, "polar", down)
+    )(x, table, filters, gs, weights_t, inverse_t)
 
 
 def local(fields, basis_spectra, support, weights, out_grad):
@@ -427,25 +521,29 @@
     forward, forward_t, inverse, inverse_t = make_tables(
         part * shares, out_grad.shape[2] * shares, shares
     )
-    gathered = lax.all_gather(out_grad[0], "azimuth", axis=0)
+    cotangent = jnp.pad(out_grad[0], ((0, 0), (0, -out_grad.shape[2] % ROWS), (0, 0)))
     pieces = fields[0].reshape(rows, part, shares, share).transpose(2, 0, 3, 1)
     spread = lax.all_to_all(pieces, "azimuth", 0, 0)
     filters = filter_rows(basis_spectra, support)
     own = lax.dynamic_slice_in_dim(weights, lax.axis_index("azimuth") * share, share, 1)
     own_t = own.reshape(taps * share, d).T
 
-    gs, sg = backward_spectra(
-        gathered, jnp.asarray(inverse), own, filters, window, rows + 2 * margin
-    )
-    low, high = to_neighbours(sg[:margin].astype(BF16), sg[margin + rows :].astype(BF16))
+    gs, sg, low, high = backward_spectra(
+        cotangent, jnp.asarray(inverse), own, filters, window, rows + 2 * margin, margin
+    )
     grad_pieces = field_gradient(sg, low, high, jnp.asarray(forward_t))
     grad_back = lax.all_to_all(grad_pieces, "azimuth", 0, 0)
 
     spread, _ = lax.optimization_barrier((spread, grad_pieces))
-    x = input_spectra(spread, jnp.asarray(forward), margin)
-    low, high = to_neighbours(x[:margin].astype(BF16), x[rows - margin :].astype(BF16))
     conv_out, weight_grad = mix(
-        x, low, high, filters, gs, own_t, jnp.asarray(inverse_t), window, out_grad.shape[2]
+        spread,
+        jnp.asarray(forward),
+        filters,
+        gs,
+        own_t,
+        jnp.asarray(inverse_t),
+        window,
+        out_grad.shape[2],
     )
     weight_grad = weight_grad.reshape(taps, share, d)
     field_grad = grad_back.transpose(1, 3, 0, 2).reshape(rows, part, channels)

time: 144 us -> 115 us (0.80)
  waiting for transfers between devices: 34.3 us -> 0.01 us
  Pallas kernels: 52.8 us -> 74 us
  between operations: 14.3 us -> 0.79 us
  starting transfers between devices: 16.3 us -> 9.65 us
  local copies, waits for them, and re-layouts: 22.6 us -> 26.6 us
    all_gather x1 -> x0, waiting for transfers between devices: 31.5 us -> none  [local(): gathered = lax.all_gather(out_grad[0], 'azimuth', axis=0)]
    pallas_call x1, Pallas kernels: 14.7 us -> 36.4 us  [backward_spectra(): pl.pallas_call(lambda *refs: back_kernel(window, *refs), grid=(outs,), in...]
    ppermute x4 -> x0, starting transfers between devices: 6.51 us -> none  [to_neighbours(): return (lax.ppermute(last, 'polar', up), lax.ppermute(first, 'polar', down))]
    unnamed x36 -> x37, local copies, waits for them, and re-layouts: 15.7 us -> 21.4 us
    pallas_call x1, Pallas kernels: 32.5 us -> 35.2 us  [mix(): pl.pallas_call(lambda *refs: mix_kernel(window, *refs), grid=(outs,), in_...]
    pallas_call x1 -> x0, Pallas kernels: 2.44 us -> none  [input_spectra(): pl.pallas_call(spectra_kernel, grid=(rows // rim,), in_specs=[pl.BlockSpe...]
    ppermute x4 -> x0, waiting for transfers between devices: 2.03 us -> none  [to_neighbours(): return (lax.ppermute(last, 'polar', up), lax.ppermute(first, 'polar', down))]
    all_gather x1 -> x0, local copies, waits for them, and re-layouts: 1.72 us -> none  [local(): gathered = lax.all_gather(out_grad[0], 'azimuth', axis=0)]
  transfers between devices with their start and end apart: 7 -> 2, of which waited for: 2 -> 0; matrix products, arithmetic and copies ran while one was open for 7% -> 5% of each run, Pallas kernels for 35% -> 65%
where the time goes in v2:
time: 115 us; the launch traced here: 113 us
  Pallas kernels  74 us (64%)
  local copies, waits for them, and re-layouts  26.6 us (23%)
  starting transfers between devices  9.65 us (8%)
  other arithmetic  2.24 us (2%)
    pallas_call x1, Pallas kernels, backward_spectra(): pl.pallas_call(lambda *refs: back_kernel(window, *refs), grid=(outs,), in...  36.4 us
    pallas_call x1, Pallas kernels, mix(): pl.pallas_call(lambda *refs: mix_kernel(window, *refs), grid=(outs,), in_...  35.2 us
    unnamed x37, local copies, waits for them, and re-layouts  21.4 us
    all_to_all x1, starting transfers between devices, local(): spread = lax.all_to_all(pieces, 'azimuth', 0, 0)  5.29 us
    all_to_all x1, starting transfers between devices, local(): grad_back = lax.all_to_all(grad_pieces, 'azimuth', 0, 0)  4.36 us
    pallas_call x1, Pallas kernels, field_gradient(): pl.pallas_call(field_grad_kernel, grid=(rows // rim,), in_specs=[pl.Block...  2.42 us
  transfers between devices with their start and end apart: 2, of which 0 were waited for; matrix products, arithmetic and copies ran while one was open for 5% of the time, Pallas kernels for 65%

profile of v2, /device:TPU:0, one launch (start us, length us, event | category | flops | bytes accessed | tf_op | source)
XLA Modules:
  0.0 113.3 jit_solution(15571991115240390289)
XLA Ops:
  0.6 0.0 copy-start
  0.6 2.0 %copy.16 = bf16[1,8,360,256]{2,3,1,0:T(8,128)(2,1)S(1)} copy(bf16[1,8,360,256]{3,2,1,0:T(8,128)(2,1)} %param.9) | data formatting | bytes 2949120 | tf_op args[0]
  2.6 1.3 %copy.29 = bf16[8,360,4,64]{1,3,0,2:T(8,128)(2,1)} copy(bf16[8,360,4,64]{1,3,2,0:T(8,128)(2,1)S(1)} %bitcast.26) | data formatting | bytes 2949120 | tf_op jit(solution)/shard_map/reshape;squeeze | solution.py:525
  3.9 0.0 copy-start.15
  3.9 0.0 copy-start.14
  4.0 5.3 %all-to-all-start = ((bf16[4,8,64,360]{3,2,1,0:T(8,128)(2,1)}), bf16[4,8,64,360]{3,2,1,0:T(8,128)(2,1)S(1)}, u32[]{:S(2)}, u32[]{:S(2)}) async-start(bf16[4,8,64,360]{3,2,1,0:T(8,128)(2,1)} %bitcast.24), calls=%async_computation | async-start | bytes 3145728 | tf_op jit(solution)/shard_map/all_to_all | solution.py:526
  9.2 0.0 copy-done.15
  9.3 0.0 copy-done.14
  9.3 0.2 broadcast_select_fusion
  9.5 1.2 %reshape.66 = bf16[9,4,10,360]{3,2,0,1:T(8,128)(2,1)} reshape(bf16[9,4,5,720]{3,2,0,1:T(8,128)(2,1)S(1)} %copy.25) | data formatting | bytes 518400 | tf_op jit(solution)/shard_map/reshape | solution.py:54
  10.7 0.0 copy-start.13
  10.7 2.0 %pad_convert_fusion.refs_3_.refs_2_ = f32[4,9,16,384]{3,2,1,0:T(8,128)} fusion(bf16[4,9,10,360]{3,2,1,0:T(8,128)(2,1)} %bitcast.27), kind=kLoop, calls=%fused_computation.1 | loop fusion | flops 221184 | bytes 1143936 | tf_op jit(solution)/shard_map/jit(_pad)/pad | solution.py:56
  12.8 0.0 copy-done.13
  12.8 0.0 copy-done
  12.9 0.0 copy-start.2
  12.9 1.2 %copy-done.2 = f32[4,9,16,384]{3,2,1,0:T(8,128)S(1)} copy-done((f32[4,9,16,384]{3,2,1,0:T(8,128)S(1)}, f32[4,9,16,384]{3,2,1,0:T(8,128)}, u32[]{:S(2)}) %copy-start.2) | copy-done | bytes 884760
  14.1 0.0 copy-start.7
  14.1 1.4 %copy-done.7 = bf16[4,768,192]{2,1,0:T(8,128)(2,1)S(1)} copy-done((bf16[4,768,192]{2,1,0:T(8,128)(2,1)S(1)}, bf16[4,768,192]{2,1,0:T(8,128)(2,1)}, u32[]{:S(2)}) %copy-start.7) | copy-done | bytes 1179672
  15.5 36.4 %shard_map.112 = (bf16[4,768,256]{2,1,0:T(8,128)(2,1)S(1)}, f32[12,64,768]{2,1,0:T(8,128)S(1)}, bf16[2,64,768]{2,1,0:T(8,128)(2,1)S(1)}, bf16[2,64,768]{2,1,0:T(8,128)(2,1)S(1)}) custom-call(bf16[4,192,256]{2,1,0:T(8,128)(2,1)S(1)} %pad.10.refs_0_, bf16[4,768,192]{2,1,0:T(8,128)(2,1)S(1)} %copy-done.7, ...), custom_call_target="tpu_custom_call" | custom-call | flops 20000000000 | bytes 10000000 | tf_op jit(solution)/shard_map/pallas_call | solution.py:213
  51.9 0.0 copy-start.9
  51.9 1.4 %copy-done.9 = f32[12,64,768]{2,1,0:T(8,128)} copy-done((f32[12,64,768]{2,1,0:T(8,128)}, f32[12,64,768]{2,1,0:T(8,128)S(1)}, u32[]{:S(2)}) %copy-start.9) | copy-done | bytes 2359320
  53.3 0.0 copy-start.11
  53.3 1.2 %copy-done.11 = bf16[4,768,256]{2,1,0:T(8,128)(2,1)} copy-done((bf16[4,768,256]{2,1,0:T(8,128)(2,1)}, bf16[4,768,256]{2,1,0:T(8,128)(2,1)S(1)}, u32[]{:S(2)}) %copy-start.11) | copy-done | bytes 1572888
  54.5 0.9 copy.21
  55.4 0.0 copy-start.5
  55.4 1.7 %copy-done.5 = bf16[4,768,360]{2,1,0:T(8,128)(2,1)S(1)} copy-done((bf16[4,768,360]{2,1,0:T(8,128)(2,1)S(1)}, bf16[4,768,360]{2,1,0:T(8,128)(2,1)}, u32[]{:S(2)}) %copy-start.5) | copy-done | bytes 2211864
  57.1 1.7 %copy-done.10 = f32[12,64,768]{2,1,0:T(8,128)S(1)} copy-done((f32[12,64,768]{2,1,0:T(8,128)S(1)}, f32[12,64,768]{2,1,0:T(8,128)}, u32[]{:S(2)}) %copy-start.10) | copy-done | bytes 2359320
  58.7 2.4 %shard_map.113 = bf16[4,8,64,360]{3,2,1,0:T(8,128)(2,1)S(1)} custom-call(f32[12,64,768]{2,1,0:T(8,128)S(1)} %copy-done.10, bf16[2,64,768]{2,1,0:T(8,128)(2,1)S(1)} %get-tuple-element.11.low_ref, bf16[2,64,768]{2,1,0:T(8,128)(2,1)S(1)} %get-tuple-element.12.high_ref, bf16[4,768,360]{2,1,0:T(8,128)(2,1)S(1)} %copy-done.5), custom_call_target="tpu_custom_call" | custom-call | flops 5000000000 | bytes 6000000 | tf_op jit(solution)/shard_map/pallas_call | solution.py:265
  61.1 0.0 copy-start.1
  61.2 1.2 %copy-done.1 = bf16[4,8,64,360]{3,2,1,0:T(8,128)(2,1)} copy-done((bf16[4,8,64,360]{3,2,1,0:T(8,128)(2,1)}, bf16[4,8,64,360]{3,2,1,0:T(8,128)(2,1)S(1)}, u32[]{:S(2)}) %copy-start.1) | copy-done | bytes 1474584
  62.3 0.0 all-to-all-done.refs_0_
  62.3 4.4 %all-to-all-start.1 = ((bf16[4,8,64,360]{3,2,1,0:T(8,128)(2,1)}), bf16[4,8,64,360]{3,2,1,0:T(8,128)(2,1)}, u32[]{:S(2)}, u32[]{:S(2)}) async-start(bf16[4,8,64,360]{3,2,1,0:T(8,128)(2,1)} %copy-done.1), calls=%async_computation.1 | async-start | bytes 3145728 | tf_op jit(solution)/shard_map/all_to_all | solution.py:535
  66.7 0.0 copy-start.3
  66.7 1.2 %copy-done.3 = f32[4,9,16,384]{3,2,1,0:T(8,128)S(1)} copy-done((f32[4,9,16,384]{3,2,1,0:T(8,128)S(1)}, f32[4,9,16,384]{3,2,1,0:T(8,128)}, u32[]{:S(2)}) %copy-start.3) | copy-done | bytes 884760
  67.8 0.0 copy-start.4
  67.9 1.0 copy-done.4
  68.8 0.0 copy-start.6
  68.8 1.6 %copy-done.6 = bf16[4,360,768]{2,1,0:T(8,128)(2,1)S(1)} copy-done((bf16[4,360,768]{2,1,0:T(8,128)(2,1)S(1)}, bf16[4,360,768]{2,1,0:T(8,128)(2,1)}, u32[]{:S(2)}) %copy-start.6) | copy-done | bytes 2211864
  70.4 0.0 copy-start.8
  70.4 1.3 %copy-done.8 = bf16[4,192,768]{2,1,0:T(8,128)(2,1)S(1)} copy-done((bf16[4,192,768]{2,1,0:T(8,128)(2,1)S(1)}, bf16[4,192,768]{2,1,0:T(8,128)(2,1)}, u32[]{:S(2)}) %copy-start.8) | copy-done | bytes 1179672
  71.7 0.0 copy-start.12
  71.7 1.4 %copy-done.12 = bf16[4,768,256]{2,1,0:T(8,128)(2,1)S(1)} copy-done((bf16[4,768,256]{2,1,0:T(8,128)(2,1)S(1)}, bf16[4,768,256]{2,1,0:T(8,128)(2,1)}, u32[]{:S(2)}) %copy-start.12) | copy-done | bytes 1572888
  73.1 35.2 %shard_map.114 = (bf16[4,180,256]{2,1,0:T(8,128)(2,1)S(1)}, f32[576,256]{1,0:T(8,128)S(1)}) custom-call(bf16[4,8,64,360]{3,2,1,0:T(8,128)(2,1)S(1)} %all-to-all-done.refs_0_, bf16[4,360,768]{2,1,0:T(8,128)(2,1)S(1)} %copy-done.6, f32[4,9,16,384]{3,2,1,0:T(8,128)S(1)} %copy-done.3, bf16[4,768,256]{2,1,0:T(8,128)(2,1)S(1)} %copy-done.12, ...), custom_call_target="tpu_custom_call" | custom-call | flops 20000000000 | bytes 10000000 | tf_op jit(solution)/shard_map/pallas_call | solution.py:473
  108.4 0.9 copy.23
  109.2 0.0 all-to-all-done.1
  109.2 1.6 %copy.22 = bf16[8,360,4,64]{1,3,2,0:T(8,128)(2,1)S(1)} copy(bf16[8,360,4,64]{1,3,0,2:T(8,128)(2,1)} %bitcast.9) | data formatting | bytes 2949120 | tf_op jit(solution)/shard_map/transpose | solution.py:549
  110.9 1.6 %copy.24 = bf16[1,8,360,256]{3,2,1,0:T(8,128)(2,1)} copy(bf16[1,8,360,256]{2,3,1,0:T(8,128)(2,1)S(1)} %bitcast.25) | data formatting | bytes 2949120
  112.5 0.8 copy.32
  (7 shorter events, 0.2 us)
Async XLA Ops:
  0.6 12.2 %copy-start = (bf16[9,256,256]{2,1,0:T(8,128)(2,1)S(1)}, bf16[9,256,256]{2,1,0:T(8,128)(2,1)}, u32[]{:S(2)}) copy-start(bf16[9,256,256]{2,1,0:T(8,128)(2,1)} %param.12) | copy-start | bytes 3538948
  3.9 5.3 %copy-start.15 = (s32[4,2]{0,1:T(2,128)S(1)}, s32[4,2]{0,1:T(2,128)}, u32[]{:S(2)}) copy-start(s32[4,2]{0,1:T(2,128)} %param.11) | copy-start | bytes 100
  3.9 5.3 %copy-start.14 = (bf16[9,4,5,720]{3,1,2,0:T(4,128)(2,1)S(1)}, bf16[9,4,5,720]{3,1,2,0:T(4,128)(2,1)}, u32[]{:S(2)}) copy-start(bf16[9,4,5,720]{3,1,2,0:T(4,128)(2,1)} %param.10) | copy-start | bytes 777604
  4.0 58.4 %all-to-all-start = ((bf16[4,8,64,360]{3,2,1,0:T(8,128)(2,1)}), bf16[4,8,64,360]{3,2,1,0:T(8,128)(2,1)S(1)}, u32[]{:S(2)}, u32[]{:S(2)}) async-start(bf16[4,8,64,360]{3,2,1,0:T(8,128)(2,1)} %bitcast.24), calls=%async_computation | async-start | bytes 3145728 | tf_op jit(solution)/shard_map/all_to_all | solution.py:526
  10.7 2.0 %copy-start.13 = (bf16[1,4,180,256]{3,1,2,0:T(4,128)(2,1)S(1)}, bf16[1,4,180,256]{3,1,2,0:T(4,128)(2,1)}, u32[]{:S(2)}) copy-start(bf16[1,4,180,256]{3,1,2,0:T(4,128)(2,1)} %param.13) | copy-start | bytes 1105924
  12.9 1.2 %copy-start.2 = (f32[4,9,16,384]{3,2,1,0:T(8,128)S(1)}, f32[4,9,16,384]{3,2,1,0:T(8,128)}, u32[]{:S(2)}) copy-start(f32[4,9,16,384]{3,2,1,0:T(8,128)} %pad_convert_fusion.refs_3_.refs_2_) | copy-start | bytes 2654212
  14.1 1.4 %copy-start.7 = (bf16[4,768,192]{2,1,0:T(8,128)(2,1)S(1)}, bf16[4,768,192]{2,1,0:T(8,128)(2,1)}, u32[]{:S(2)}) copy-start(bf16[4,768,192]{2,1,0:T(8,128)(2,1)} %constant.23.clone.refs_1_) | copy-start | bytes 3538948
  51.9 1.4 %copy-start.9 = (f32[12,64,768]{2,1,0:T(8,128)}, f32[12,64,768]{2,1,0:T(8,128)S(1)}, u32[]{:S(2)}) copy-start(f32[12,64,768]{2,1,0:T(8,128)S(1)} %get-tuple-element.10.sg_ref) | copy-start | bytes 7077892
  53.3 1.2 %copy-start.11 = (bf16[4,768,256]{2,1,0:T(8,128)(2,1)}, bf16[4,768,256]{2,1,0:T(8,128)(2,1)S(1)}, u32[]{:S(2)}) copy-start(bf16[4,768,256]{2,1,0:T(8,128)(2,1)S(1)} %get-tuple-element.14.refs_3_) | copy-start | bytes 4718596
  55.4 1.7 %copy-start.5 = (bf16[4,768,360]{2,1,0:T(8,128)(2,1)S(1)}, bf16[4,768,360]{2,1,0:T(8,128)(2,1)}, u32[]{:S(2)}) copy-start(bf16[4,768,360]{2,1,0:T(8,128)(2,1)} %constant.24.clone.table_ref) | copy-start | bytes 6635524
  57.1 1.7 %copy-start.10 = (f32[12,64,768]{2,1,0:T(8,128)S(1)}, f32[12,64,768]{2,1,0:T(8,128)}, u32[]{:S(2)}) copy-start(f32[12,64,768]{2,1,0:T(8,128)} %copy-done.9) | copy-start | bytes 7077892
  61.1 1.2 %copy-start.1 = (bf16[4,8,64,360]{3,2,1,0:T(8,128)(2,1)}, bf16[4,8,64,360]{3,2,1,0:T(8,128)(2,1)S(1)}, u32[]{:S(2)}) copy-start(bf16[4,8,64,360]{3,2,1,0:T(8,128)(2,1)S(1)} %shard_map.113) | copy-start | bytes 4423684
  62.3 46.9 %all-to-all-start.1 = ((bf16[4,8,64,360]{3,2,1,0:T(8,128)(2,1)}), bf16[4,8,64,360]{3,2,1,0:T(8,128)(2,1)}, u32[]{:S(2)}, u32[]{:S(2)}) async-start(bf16[4,8,64,360]{3,2,1,0:T(8,128)(2,1)} %copy-done.1), calls=%async_computation.1 | async-start | bytes 3145728 | tf_op jit(solution)/shard_map/all_to_all | solution.py:535
  66.7 1.2 %copy-start.3 = (f32[4,9,16,384]{3,2,1,0:T(8,128)S(1)}, f32[4,9,16,384]{3,2,1,0:T(8,128)}, u32[]{:S(2)}) copy-start(f32[4,9,16,384]{3,2,1,0:T(8,128)} %pad_convert_fusion.refs_3_.refs_2_) | copy-start | bytes 2654212
  67.8 1.0 copy-start.4
  68.8 1.6 %copy-start.6 = (bf16[4,360,768]{2,1,0:T(8,128)(2,1)S(1)}, bf16[4,360,768]{2,1,0:T(8,128)(2,1)}, u32[]{:S(2)}) copy-start(bf16[4,360,768]{2,1,0:T(8,128)(2,1)} %constant.25.clone.refs_1_) | copy-start | bytes 6635524
  70.4 1.3 %copy-start.8 = (bf16[4,192,768]{2,1,0:T(8,128)(2,1)S(1)}, bf16[4,192,768]{2,1,0:T(8,128)(2,1)}, u32[]{:S(2)}) copy-start(bf16[4,192,768]{2,1,0:T(8,128)(2,1)} %constant.26.clone.refs_5_) | copy-start | bytes 3538948
  71.7 1.4 %copy-start.12 = (bf16[4,768,256]{2,1,0:T(8,128)(2,1)S(1)}, bf16[4,768,256]{2,1,0:T(8,128)(2,1)}, u32[]{:S(2)}) copy-start(bf16[4,768,256]{2,1,0:T(8,128)(2,1)} %copy-done.11) | copy-start | bytes 4718596

commit v3 on v2

--- a/solution.py
+++ b/solution.py
@@ -60,16 +60,10 @@
     return pl.BlockSpec(shape, lambda i: (0,) * len(shape))
 
 
-def params():
-    return pltpu.CompilerParams(
-        dimension_semantics=("arbitrary",), vmem_limit_bytes=40 * 1024 * 1024
-    )
-
-
 def remote_params(identity):
     return pltpu.CompilerParams(
         dimension_semantics=("arbitrary",),
-        vmem_limit_bytes=40 * 1024 * 1024,
+        vmem_limit_bytes=30 * 1024 * 1024,
         collective_id=identity,
         has_side_effects=True,
     )
@@ -102,13 +96,14 @@
     return low, high
 
 
-def back_kernel(window, og_ref, inv_ref, w_ref, mk_ref, gs_ref, sg_ref, low_ref, high_ref,
-                mg_ref, og_all, rim_send, rim_recv,
-                og_out_sem, og_in_sem, rim_out_sem, rim_in_sem):
+def back_kernel(window, og_ref, x_ref, inv_ref, w_ref, mk_ref, table_ref,
+                gs_ref, spread_ref, out_ref,
+                sg_ref, mg_ref, og_all, x_all, rim_send, rim_recv,
+                x_out_sem, x_in_sem, og_out_sem, og_in_sem, rim_out_sem, rim_in_sem):
     o = pl.program_id(0)
     shares, outs = og_all.shape[:2]
     taps, share, columns = mg_ref.shape
-    rim = low_ref.shape[0]
+    rim = rim_send.shape[1]
     me = lax.axis_index("azimuth")
     bands = lax.axis_size("polar")
 
@@ -120,6 +115,18 @@
             dst_ref=og_all.at[at, row],
             send_sem=og_out_sem.at[step, row],
             recv_sem=og_in_sem.at[at, row],
+            device_id={"azimuth": other},
+            device_id_type=pl.DeviceIdType.MESH,
+        )
+
+    def x_copy(step, arriving):
+        other = lax.rem(me + step, shares)
+        at = other if arriving else me
+        return pltpu.make_async_remote_copy(
+            src_ref=x_ref.at[other],
+            dst_ref=x_all.at[at],
+            send_sem=x_out_sem.at[step],
+            recv_sem=x_in_sem.at[at],
             device_id={"azimuth": other},
             device_id_type=pl.DeviceIdType.MESH,
         )
@@ -145,6 +152,9 @@
         for row in range(outs):
             for step in range(1, shares):
                 og_copy(row, step, False).start()
+        for step in range(1, shares):
+            x_copy(step, False).start()
+        spread_ref[me] = x_ref[me]
 
     wide = columns // 2
     block = min(ROWS, share)
@@ -196,8 +206,20 @@
         for copy in copies:
             copy.wait_recv()
         low, high = rim_values(rim_recv)
-        low_ref[...] = low.astype(BF16)
-        high_ref[...] = high.astype(BF16)
+        total_rows = sg_ref.shape[0]
+        sg_ref[rim : 2 * rim] += low
+        sg_ref[total_rows - 2 * rim : total_rows - rim] += high
+        for first in range(0, total_rows - 2 * rim, rim):
+            value = sg_ref[rim + first : 2 * rim + first].astype(BF16)
+            value = value.reshape(rim * share, columns)
+            for s in range(shares):
+                piece = jnp.dot(value, table_ref[s], preferred_element_type=F32)
+                out_ref[s, first : first + rim] = piece.astype(BF16).reshape(rim, share, -1)
+        for step in range(1, shares):
+            other = lax.rem(me + step, shares)
+            x_copy(step, True).wait_recv()
+            spread_ref[other] = x_all[other]
+            x_copy(step, False).wait_send()
         for copy in copies:
             copy.wait_send()
         for row in range(outs):
@@ -205,37 +227,43 @@
                 og_copy(row, step, False).wait_send()
 
 
-def backward_spectra(cotangent, inverse, weights, filters, window, rows_total, rim):
+def backward(cotangent, pieces, inverse, weights, filters, table, window):
     outs, padded, d = cotangent.shape
     shares, columns, _ = inverse.shape
     taps, share, _ = weights.shape
+    rim = window // 2
+    rows_total = pieces.shape[1] + 2 * rim
     dma = pltpu.SemaphoreType.DMA
     return pl.pallas_call(
         lambda *refs: back_kernel(window, *refs),
         grid=(outs,),
         in_specs=[
             whole(cotangent.shape),
+            whole(pieces.shape),
             whole(inverse.shape),
             whole(weights.shape),
             pl.BlockSpec((1,) + filters.shape[1:], lambda i: (i, 0, 0, 0)),
+            whole(table.shape),
         ],
         out_specs=[
             pl.BlockSpec((1, columns, d), lambda i: (i, 0, 0)),
-            whole((rows_total, share, columns)),
-            whole((rim, share, columns)),
-            whole((rim, share, columns)),
+            whole(pieces.shape),
+            whole(pieces.shape),
         ],
         out_shape=[
             jax.ShapeDtypeStruct((outs, columns, d), BF16),
-            jax.ShapeDtypeStruct((rows_total, share, columns), F32),
-            jax.ShapeDtypeStruct((rim, share, columns), BF16),
-            jax.ShapeDtypeStruct((rim, share, columns), BF16),
+            jax.ShapeDtypeStruct(pieces.shape, BF16),
+            jax.ShapeDtypeStruct(pieces.shape, BF16),
         ],
         scratch_shapes=[
+            pltpu.VMEM((rows_total, share, columns), F32),
             pltpu.VMEM((taps, share, columns), F32),
             pltpu.VMEM((shares, outs, padded, d), BF16),
+            pltpu.VMEM(pieces.shape, BF16),
             pltpu.VMEM((2, rim, share, columns), BF16),
             pltpu.VMEM((2, rim, share, columns), BF16),
+            dma((shares,)),
+            dma((shares,)),
             dma((shares, outs)),
             dma((shares, outs)),
             dma((2,)),
@@ -243,39 +271,7 @@
         ],
         compiler_params=remote_params(1),
         cost_estimate=cost(2e10, 1e7),
-    )(cotangent, inverse, weights, filters)
-
-
-def field_grad_kernel(sg_ref, low_ref, high_ref, table_ref, out_ref):
-    i = pl.program_id(0)
-    last = pl.num_programs(0) - 1
-    rows, share, columns = sg_ref.shape
-    low = jnp.where(i == 0, low_ref[...].astype(F32), 0.0)
-    high = jnp.where(i == last, high_ref[...].astype(F32), 0.0)
-    value = (sg_ref[...] + low + high).astype(BF16).reshape(rows * share, columns)
-    for s in range(table_ref.shape[0]):
-        piece = jnp.dot(value, table_ref[s], preferred_element_type=F32)
-        out_ref[s] = piece.astype(BF16).reshape(rows, share, piece.shape[1])
-
-
-def field_gradient(sg, low, high, table):
-    rim, share, columns = low.shape
-    rows = sg.shape[0] - 2 * rim
-    shares, _, part = table.shape
-    return pl.pallas_call(
-        field_grad_kernel,
-        grid=(rows // rim,),
-        in_specs=[
-            pl.BlockSpec((rim, share, columns), lambda i: (i + 1, 0, 0)),
-            whole(low.shape),
-            whole(high.shape),
-            whole(table.shape),
-        ],
-        out_specs=pl.BlockSpec((shares, rim, share, part), lambda i: (0, i, 0, 0)),
-        out_shape=jax.ShapeDtypeStruct((shares, rows, share, part), BF16),
-        compiler_params=params(),
-        cost_estimate=cost(5e9, 6e6),
-    )(sg, low, high, table)
+    )(cotangent, pieces, inverse, weights, filters, table)
 
 
 def mix_kernel(window, x_ref, table_ref, mk_ref, gs_ref, wt_ref, inv_ref,
@@ -514,7 +510,6 @@
 def local(fields, basis_spectra, support, weights, out_grad):
     shares = lax.axis_size("azimuth")
     window = basis_spectra.shape[2]
-    margin = window // 2
     _, rows, part, channels = fields.shape
     share = channels // shares
     taps, _, d = weights.shape
@@ -523,18 +518,15 @@
     )
     cotangent = jnp.pad(out_grad[0], ((0, 0), (0, -out_grad.shape[2] % ROWS), (0, 0)))
     pieces = fields[0].reshape(rows, part, shares, share).transpose(2, 0, 3, 1)
-    spread = lax.all_to_all(pieces, "azimuth", 0, 0)
     filters = filter_rows(basis_spectra, support)
     own = lax.dynamic_slice_in_dim(weights, lax.axis_index("azimuth") * share, share, 1)
     own_t = own.reshape(taps * share, d).T
 
-    gs, sg, low, high = backward_spectra(
-        cotangent, jnp.asarray(inverse), own, filters, window, rows + 2 * margin, margin
-    )
-    grad_pieces = field_gradient(sg, low, high, jnp.asarray(forward_t))
+    gs, spread, grad_pieces = backward(
+        cotangent, pieces, jnp.asarray(inverse), own, filters, jnp.asarray(forward_t), window
+    )
     grad_back = lax.all_to_all(grad_pieces, "azimuth", 0, 0)
 
-    spread, _ = lax.optimization_barrier((spread, grad_pieces))
     conv_out, weight_grad = mix(
         spread,
         jnp.asarray(forward),

time: 115 us -> 106 us (0.922)
  starting transfers between devices: 9.65 us -> 4.48 us
  local copies, waits for them, and re-layouts: 26.6 us -> 22 us
  Pallas kernels: 74 us -> 75.4 us
    all_to_all x1 -> x0, starting transfers between devices: 5.29 us -> none  [local(): spread = lax.all_to_all(pieces, 'azimuth', 0, 0)]
    unnamed x37 -> x31, local copies, waits for them, and re-layouts: 21.4 us -> 17.2 us
    pallas_call x2 -> x1, Pallas kernels: 38.8 us -> 40.3 us  [backward(): pl.pallas_call(lambda *refs: back_kernel(window, *refs), grid=(outs,), in...]
  transfers between devices with their start and end apart: 2 -> 1, of which waited for: 0 -> 0; matrix products, arithmetic and copies ran while one was open for 5% -> 1% of each run, Pallas kernels for 65% -> 34%
where the time goes in v3:
time: 106 us; the launch traced here: 105 us
  Pallas kernels  75.4 us (71%)
  local copies, waits for them, and re-layouts  22 us (21%)
  starting transfers between devices  4.48 us (4%)
  other arithmetic  2.12 us (2%)
    pallas_call x1, Pallas kernels, backward(): pl.pallas_call(lambda *refs: back_kernel(window, *refs), grid=(outs,), in...  40.3 us
    pallas_call x1, Pallas kernels, mix(): pl.pallas_call(lambda *refs: mix_kernel(window, *refs), grid=(outs,), in_...  35.1 us
    unnamed x31, local copies, waits for them, and re-layouts  17.2 us
    all_to_all x1, starting transfers between devices, local(): grad_back = lax.all_to_all(grad_pieces, 'azimuth', 0, 0)  4.48 us
  transfers between devices with their start and end apart: 1, of which 0 were waited for; matrix products, arithmetic and copies ran while one was open for 1% of the time, Pallas kernels for 34%

profile of v3, /device:TPU:0, one launch (start us, length us, event | category | flops | bytes accessed | tf_op | source)
XLA Modules:
  0.0 104.8 jit_solution(3527870578457312813)
XLA Ops:
  0.6 0.0 copy-start
  0.6 0.8 slice_bitcast_fusion.1
  1.5 1.1 %broadcast_select_fusion = bf16[9,4,5,720]{3,1,2,0:T(4,128)(2,1)S(1)} fusion(bf16[9,4,5,720]{3,1,2,0:T(4,128)(2,1)} %param.10, pred[4,5]{0,1:T(8,128)(4,1)S(1)} %fusion), kind=kLoop, calls=%fused_computation.3 | loop fusion | flops 129600 | bytes 518420 | tf_op jit(solution)/shard_map/jit(_where)/select_n | solution.py:53
  2.6 0.0 copy-start.11
  2.7 0.4 reshape.66
  3.1 1.0 pad_convert_fusion.refs_4_.refs_2_
  4.1 0.0 copy-done.11
  4.1 1.6 %copy.17 = bf16[1,8,360,256]{2,3,1,0:T(8,128)(2,1)} copy(bf16[1,8,360,256]{3,2,1,0:T(8,128)(2,1)S(1)} %copy-done.11) | data formatting | bytes 2949120 | tf_op args[0]
  5.7 0.0 copy-start.12
  5.7 1.6 %copy.29 = bf16[8,360,4,64]{1,3,0,2:T(8,128)(2,1)S(1)} copy(bf16[8,360,4,64]{1,3,2,0:T(8,128)(2,1)} %bitcast.26) | data formatting | bytes 2949120 | tf_op jit(solution)/shard_map/reshape;squeeze | solution.py:520
  7.3 0.0 copy-done.12
  7.4 0.0 copy-done
  7.5 0.0 copy-start.1
  7.5 1.2 %copy-done.1 = f32[4,9,16,384]{3,2,1,0:T(8,128)S(1)} copy-done((f32[4,9,16,384]{3,2,1,0:T(8,128)S(1)}, f32[4,9,16,384]{3,2,1,0:T(8,128)}, u32[]{:S(2)}) %copy-start.1) | copy-done | bytes 884760
  8.6 0.0 copy-start.3
  8.6 1.7 %copy-done.3 = bf16[4,768,360]{2,1,0:T(8,128)(2,1)S(1)} copy-done((bf16[4,768,360]{2,1,0:T(8,128)(2,1)S(1)}, bf16[4,768,360]{2,1,0:T(8,128)(2,1)}, u32[]{:S(2)}) %copy-start.3) | copy-done | bytes 2211864
  10.3 0.0 copy-start.5
  10.3 1.4 %copy-done.5 = bf16[4,768,192]{2,1,0:T(8,128)(2,1)S(1)} copy-done((bf16[4,768,192]{2,1,0:T(8,128)(2,1)S(1)}, bf16[4,768,192]{2,1,0:T(8,128)(2,1)}, u32[]{:S(2)}) %copy-start.5) | copy-done | bytes 1179672
  11.7 40.3 %shard_map.112 = (bf16[4,768,256]{2,1,0:T(8,128)(2,1)S(1)}, bf16[4,8,64,360]{3,2,1,0:T(8,128)(2,1)S(1)}, bf16[4,8,64,360]{3,2,1,0:T(8,128)(2,1)}) custom-call(bf16[4,192,256]{2,1,0:T(8,128)(2,1)S(1)} %pad.10.refs_0_, bf16[4,8,64,360]{3,2,1,0:T(8,128)(2,1)S(1)} %bitcast.20, bf16[4,768,192]{2,1,0:T(8,128)(2,1)S(1)} %copy-done.5, ...), custom_call_target="tpu_custom_call" | custom-call | flops 20000000000 | bytes 10000000 | tf_op jit(solution)/shard_map/pallas_call | solution.py:237
  52.0 0.0 copy-start.7
  52.0 1.2 %copy-done.7 = bf16[4,768,256]{2,1,0:T(8,128)(2,1)} copy-done((bf16[4,768,256]{2,1,0:T(8,128)(2,1)}, bf16[4,768,256]{2,1,0:T(8,128)(2,1)S(1)}, u32[]{:S(2)}) %copy-start.7) | copy-done | bytes 1572888
  53.2 0.0 copy-start.9
  53.2 1.2 %copy-done.9 = bf16[4,8,64,360]{3,2,1,0:T(8,128)(2,1)} copy-done((bf16[4,8,64,360]{3,2,1,0:T(8,128)(2,1)}, bf16[4,8,64,360]{3,2,1,0:T(8,128)(2,1)S(1)}, u32[]{:S(2)}) %copy-start.9) | copy-done | bytes 1474584
  54.3 0.0 copy-start.2
  54.3 4.5 %all-to-all-start = ((bf16[4,8,64,360]{3,2,1,0:T(8,128)(2,1)}), bf16[4,8,64,360]{3,2,1,0:T(8,128)(2,1)}, u32[]{:S(2)}, u32[]{:S(2)}) async-start(bf16[4,8,64,360]{3,2,1,0:T(8,128)(2,1)} %get-tuple-element.11), calls=%async_computation | async-start | bytes 3145728 | tf_op jit(solution)/shard_map/all_to_all | solution.py:528
  58.8 0.2 copy.21
  59.0 0.0 copy-done.2
  59.0 0.0 copy-start.4
  59.1 1.6 %copy-done.4 = bf16[4,360,768]{2,1,0:T(8,128)(2,1)S(1)} copy-done((bf16[4,360,768]{2,1,0:T(8,128)(2,1)S(1)}, bf16[4,360,768]{2,1,0:T(8,128)(2,1)}, u32[]{:S(2)}) %copy-start.4) | copy-done | bytes 2211864
  60.7 0.0 copy-start.6
  60.7 1.3 %copy-done.6 = bf16[4,192,768]{2,1,0:T(8,128)(2,1)S(1)} copy-done((bf16[4,192,768]{2,1,0:T(8,128)(2,1)S(1)}, bf16[4,192,768]{2,1,0:T(8,128)(2,1)}, u32[]{:S(2)}) %copy-start.6) | copy-done | bytes 1179672
  61.9 0.0 copy-start.8
  61.9 1.4 %copy-done.8 = bf16[4,768,256]{2,1,0:T(8,128)(2,1)S(1)} copy-done((bf16[4,768,256]{2,1,0:T(8,128)(2,1)S(1)}, bf16[4,768,256]{2,1,0:T(8,128)(2,1)}, u32[]{:S(2)}) %copy-start.8) | copy-done | bytes 1572888
  63.3 0.0 copy-start.10
  63.4 1.4 %copy-done.10 = bf16[4,8,64,360]{3,2,1,0:T(8,128)(2,1)S(1)} copy-done((bf16[4,8,64,360]{3,2,1,0:T(8,128)(2,1)S(1)}, bf16[4,8,64,360]{3,2,1,0:T(8,128)(2,1)}, u32[]{:S(2)}) %copy-start.10) | copy-done | bytes 1474584
  64.8 35.1 %shard_map.113 = (bf16[4,180,256]{2,1,0:T(8,128)(2,1)S(1)}, f32[576,256]{1,0:T(8,128)S(1)}) custom-call(bf16[4,8,64,360]{3,2,1,0:T(8,128)(2,1)S(1)} %copy-done.10, bf16[4,360,768]{2,1,0:T(8,128)(2,1)S(1)} %copy-done.4, f32[4,9,16,384]{3,2,1,0:T(8,128)S(1)} %copy-done.2, bf16[4,768,256]{2,1,0:T(8,128)(2,1)S(1)} %copy-done.8, bf16[256,576]{1,0:T(8,128)(2,1)S(1)} %bitcast.24, ...), custom_call_target="tpu_custom_call" | custom-call | flops 20000000000 | bytes 10000000 | tf_op jit(solution)/shard_map/pallas_call | solution.py:469
  99.9 0.9 copy.23
  100.8 0.0 all-to-all-done
  100.8 1.6 %copy.22 = bf16[8,360,4,64]{1,3,2,0:T(8,128)(2,1)S(1)} copy(bf16[8,360,4,64]{1,3,0,2:T(8,128)(2,1)} %bitcast.9) | data formatting | bytes 2949120 | tf_op jit(solution)/shard_map/transpose | solution.py:541
  102.4 1.6 %copy.24 = bf16[1,8,360,256]{3,2,1,0:T(8,128)(2,1)} copy(bf16[1,8,360,256]{2,3,1,0:T(8,128)(2,1)S(1)} %bitcast.25) | data formatting | bytes 2949120
  104.0 0.8 copy.32
  (5 shorter events, 0.2 us)
Async XLA Ops:
  0.6 6.8 %copy-start = (bf16[9,256,256]{2,1,0:T(8,128)(2,1)S(1)}, bf16[9,256,256]{2,1,0:T(8,128)(2,1)}, u32[]{:S(2)}) copy-start(bf16[9,256,256]{2,1,0:T(8,128)(2,1)} %param.12) | copy-start | bytes 3538948
  2.6 1.5 %copy-start.11 = (bf16[1,8,360,256]{3,2,1,0:T(8,128)(2,1)S(1)}, bf16[1,8,360,256]{3,2,1,0:T(8,128)(2,1)}, u32[]{:S(2)}) copy-start(bf16[1,8,360,256]{3,2,1,0:T(8,128)(2,1)} %param.9) | copy-start | bytes 4423684
  5.7 1.7 %copy-start.12 = (bf16[1,4,180,256]{3,1,2,0:T(4,128)(2,1)S(1)}, bf16[1,4,180,256]{3,1,2,0:T(4,128)(2,1)}, u32[]{:S(2)}) copy-start(bf16[1,4,180,256]{3,1,2,0:T(4,128)(2,1)} %param.13) | copy-start | bytes 1105924
  7.5 1.2 %copy-start.1 = (f32[4,9,16,384]{3,2,1,0:T(8,128)S(1)}, f32[4,9,16,384]{3,2,1,0:T(8,128)}, u32[]{:S(2)}) copy-start(f32[4,9,16,384]{3,2,1,0:T(8,128)} %pad_convert_fusion.refs_4_.refs_2_) | copy-start | bytes 2654212
  8.6 1.7 %copy-start.3 = (bf16[4,768,360]{2,1,0:T(8,128)(2,1)S(1)}, bf16[4,768,360]{2,1,0:T(8,128)(2,1)}, u32[]{:S(2)}) copy-start(bf16[4,768,360]{2,1,0:T(8,128)(2,1)} %constant.24.clone.refs_5_) | copy-start | bytes 6635524
  10.3 1.4 %copy-start.5 = (bf16[4,768,192]{2,1,0:T(8,128)(2,1)S(1)}, bf16[4,768,192]{2,1,0:T(8,128)(2,1)}, u32[]{:S(2)}) copy-start(bf16[4,768,192]{2,1,0:T(8,128)(2,1)} %constant.23.clone.refs_2_) | copy-start | bytes 3538948
  52.0 1.2 %copy-start.7 = (bf16[4,768,256]{2,1,0:T(8,128)(2,1)}, bf16[4,768,256]{2,1,0:T(8,128)(2,1)S(1)}, u32[]{:S(2)}) copy-start(bf16[4,768,256]{2,1,0:T(8,128)(2,1)S(1)} %get-tuple-element.9.refs_3_) | copy-start | bytes 4718596
  53.2 1.2 %copy-start.9 = (bf16[4,8,64,360]{3,2,1,0:T(8,128)(2,1)}, bf16[4,8,64,360]{3,2,1,0:T(8,128)(2,1)S(1)}, u32[]{:S(2)}) copy-start(bf16[4,8,64,360]{3,2,1,0:T(8,128)(2,1)S(1)} %get-tuple-element.8.refs_0_) | copy-start | bytes 4423684
  54.3 4.7 %copy-start.2 = (f32[4,9,16,384]{3,2,1,0:T(8,128)S(1)}, f32[4,9,16,384]{3,2,1,0:T(8,128)}, u32[]{:S(2)}) copy-start(f32[4,9,16,384]{3,2,1,0:T(8,128)} %pad_convert_fusion.refs_4_.refs_2_) | copy-start | bytes 2654212
  54.3 46.4 %all-to-all-start = ((bf16[4,8,64,360]{3,2,1,0:T(8,128)(2,1)}), bf16[4,8,64,360]{3,2,1,0:T(8,128)(2,1)}, u32[]{:S(2)}, u32[]{:S(2)}) async-start(bf16[4,8,64,360]{3,2,1,0:T(8,128)(2,1)} %get-tuple-element.11), calls=%async_computation | async-start | bytes 3145728 | tf_op jit(solution)/shard_map/all_to_all | solution.py:528
  59.0 1.6 %copy-start.4 = (bf16[4,360,768]{2,1,0:T(8,128)(2,1)S(1)}, bf16[4,360,768]{2,1,0:T(8,128)(2,1)}, u32[]{:S(2)}) copy-start(bf16[4,360,768]{2,1,0:T(8,128)(2,1)} %constant.25.clone.refs_1_) | copy-start | bytes 6635524
  60.7 1.3 %copy-start.6 = (bf16[4,192,768]{2,1,0:T(8,128)(2,1)S(1)}, bf16[4,192,768]{2,1,0:T(8,128)(2,1)}, u32[]{:S(2)}) copy-start(bf16[4,192,768]{2,1,0:T(8,128)(2,1)} %constant.26.clone.refs_5_) | copy-start | bytes 3538948
  61.9 1.4 %copy-start.8 = (bf16[4,768,256]{2,1,0:T(8,128)(2,1)S(1)}, bf16[4,768,256]{2,1,0:T(8,128)(2,1)}, u32[]{:S(2)}) copy-start(bf16[4,768,256]{2,1,0:T(8,128)(2,1)} %copy-done.7) | copy-start | bytes 4718596
  63.3 1.4 %copy-start.10 = (bf16[4,8,64,360]{3,2,1,0:T(8,128)(2,1)S(1)}, bf16[4,8,64,360]{3,2,1,0:T(8,128)(2,1)}, u32[]{:S(2)}) copy-start(bf16[4,8,64,360]{3,2,1,0:T(8,128)(2,1)} %copy-done.9) | copy-start | bytes 4423684

commit v4 on v3

--- a/solution.py
+++ b/solution.py
@@ -274,8 +274,8 @@
     )(cotangent, pieces, inverse, weights, filters, table)
 
 
-def mix_kernel(window, x_ref, table_ref, mk_ref, gs_ref, wt_ref, inv_ref,
-               conv_ref, wg_ref, ext_ref, mixed_ref, total_ref,
+def mix_kernel(window, fg_ref, x_ref, table_ref, mk_ref, gs_ref, wt_ref, inv_ref,
+               conv_ref, wg_ref, back_ref, fg_all, fg_out_sem, fg_in_sem, ext_ref, mixed_ref, total_ref,
                conv_send, conv_recv, piece_send, piece_recv, sums, rim_send, rim_recv,
                rim_out_sem, rim_in_sem, conv_out_sem, conv_in_sem, piece_out_sem, piece_in_sem, sum_out_sem, sum_in_sem):
     o = pl.program_id(0)
@@ -300,6 +300,18 @@
         other = lax.rem(rank + step, count)
         return other, {"ens": lax.div(other, bands), "polar": lax.rem(other, bands)}
 
+    def fg_copy(step, arriving):
+        other, device = across(step)
+        at = other if arriving else me
+        return pltpu.make_async_remote_copy(
+            src_ref=fg_ref.at[other],
+            dst_ref=fg_all.at[at],
+            send_sem=fg_out_sem.at[step],
+            recv_sem=fg_in_sem.at[at],
+            device_id=device,
+            device_id_type=pl.DeviceIdType.MESH,
+        )
+
     def conv_copy(row, step):
         other, device = across(step)
         return pltpu.make_async_remote_copy(
@@ -358,6 +370,9 @@
                 barrier, inc=1, device_id=along(step)[1], device_id_type=pl.DeviceIdType.MESH
             )
         pl.semaphore_wait(barrier, shares + count - 2)
+        for step in range(1, shares):
+            fg_copy(step, False).start()
+        back_ref[me] = fg_ref[me]
 
         def spectra(first):
             value = None
@@ -437,6 +452,11 @@
         sums[rank] = whole_sum.astype(BF16)
         for step in range(1, count):
             sum_copy(step, None).start()
+        for step in range(1, shares):
+            other = across(step)[0]
+            fg_copy(step, True).wait_recv()
+            back_ref[other] = fg_all[other]
+            fg_copy(step, False).wait_send()
         for row in range(outs):
             for step in range(1, shares):
                 conv_arrival(row, step).wait_recv()
@@ -456,7 +476,7 @@
             sum_copy(step, None).wait_send()
 
 
-def mix(x, table, filters, gs, weights_t, inverse_t, window, part):
+def mix(pieces, x, table, filters, gs, weights_t, inverse_t, window, part):
     _, rows, share, _ = x.shape
     columns = table.shape[2]
     rim = window // 2
@@ -470,6 +490,7 @@
         lambda *refs: mix_kernel(window, *refs),
         grid=(outs,),
         in_specs=[
+            whole(pieces.shape),
             whole(x.shape),
             whole(table.shape),
             pl.BlockSpec((1,) + filters.shape[1:], lambda i: (i, 0, 0, 0)),
@@ -477,12 +498,16 @@
             whole(weights_t.shape),
             whole(inverse_t.shape),
         ],
-        out_specs=[whole((outs, part, d)), whole((taps * share, d))],
+        out_specs=[whole((outs, part, d)), whole((taps * share, d)), whole(pieces.shape)],
         out_shape=[
             jax.ShapeDtypeStruct((outs, part, d), BF16),
             jax.ShapeDtypeStruct((taps * share, d), F32),
+            jax.ShapeDtypeStruct(pieces.shape, BF16),
         ],
         scratch_shapes=[
+            pltpu.VMEM(pieces.shape, BF16),
+            dma((shares,)),
+            dma((shares,)),
             pltpu.VMEM((rows + 2 * rim, share, columns), F32),
             pltpu.VMEM((taps, share, columns), BF16),
             pltpu.VMEM((count * piece, d), F32),
@@ -504,7 +529,7 @@
         ],
         compiler_params=remote_params(0),
         cost_estimate=cost(2e10, 1e7),
-    )(x, table, filters, gs, weights_t, inverse_t)
+    )(pieces, x, table, filters, gs, weights_t, inverse_t)
 
 
 def local(fields, basis_spectra, support, weights, out_grad):
@@ -525,9 +550,9 @@
     gs, spread, grad_pieces = backward(
         cotangent, pieces, jnp.asarray(inverse), own, filters, jnp.asarray(forward_t), window
     )
-    grad_back = lax.all_to_all(grad_pieces, "azimuth", 0, 0)
-
-    conv_out, weight_grad = mix(
+
+    conv_out, weight_grad, grad_back = mix(
+        grad_pieces,
         spread,
         jnp.asarray(forward),
         filters,

time: 106 us -> 97.5 us (0.920)
  local copies, waits for them, and re-layouts: 22 us -> 15 us
  Pallas kernels: 75.4 us -> 80.2 us
  starting transfers between devices: 4.48 us -> 0 us
    unnamed x31 -> x19, local copies, waits for them, and re-layouts: 17.2 us -> 9.61 us
    pallas_call x1, Pallas kernels: 35.1 us -> 41.1 us  [mix(): pl.pallas_call(lambda *refs: mix_kernel(window, *refs), grid=(outs,), in_...]
    all_to_all x1 -> x0, starting transfers between devices: 4.48 us -> none  [local(): grad_back = lax.all_to_all(grad_pieces, 'azimuth', 0, 0)]
    pallas_call x1, Pallas kernels: 40.3 us -> 39.1 us  [backward(): pl.pallas_call(lambda *refs: back_kernel(window, *refs), grid=(outs,), in...]
  transfers between devices with their start and end apart: 1 -> 0, of which waited for: 0 -> 0; matrix products, arithmetic and copies ran while one was open for 1% -> 0% of each run, Pallas kernels for 34% -> 0%
where the time goes in v4:
time: 97.5 us; the launch traced here: 97.2 us
  Pallas kernels  80.2 us (82%)
  local copies, waits for them, and re-layouts  15 us (15%)
  other arithmetic  1.26 us (1%)
    pallas_call x1, Pallas kernels, mix(): pl.pallas_call(lambda *refs: mix_kernel(window, *refs), grid=(outs,), in_...  41.1 us
    pallas_call x1, Pallas kernels, backward(): pl.pallas_call(lambda *refs: back_kernel(window, *refs), grid=(outs,), in...  39.1 us
    unnamed x19, local copies, waits for them, and re-layouts  9.61 us

profile of v4, /device:TPU:0, one launch (start us, length us, event | category | flops | bytes accessed | tf_op | source)
XLA Modules:
  0.0 97.2 jit_solution(9504843747100575290)
XLA Ops:
  0.6 0.0 copy-start
  0.6 0.8 slice_bitcast_fusion.1
  1.5 0.0 copy-start.6
  1.5 1.2 %broadcast_select_fusion = bf16[9,4,5,720]{3,1,2,0:T(4,128)(2,1)S(1)} fusion(bf16[9,4,5,720]{3,1,2,0:T(4,128)(2,1)} %param.10, pred[4,5]{0,1:T(8,128)(4,1)S(1)} %fusion), kind=kLoop, calls=%fused_computation.3 | loop fusion | flops 129600 | bytes 518420 | tf_op jit(solution)/shard_map/jit(_where)/select_n | solution.py:53
  2.7 1.2 %reshape.66 = bf16[9,4,10,360]{3,2,0,1:T(8,128)(2,1)} reshape(bf16[9,4,5,720]{3,2,0,1:T(8,128)(2,1)S(1)} %copy.25) | data formatting | bytes 518400 | tf_op jit(solution)/shard_map/reshape | solution.py:54
  3.9 0.0 copy-done
  3.9 0.2 copy.21
  4.1 0.0 copy-start.5
  4.2 0.0 copy-done.6
  4.2 0.9 copy-done.5
  5.2 0.1 pad_convert_fusion.refs_4_.refs_3_
  5.2 2.6 %copy.17 = bf16[1,8,360,256]{2,3,1,0:T(8,128)(2,1)} copy(bf16[1,8,360,256]{3,2,1,0:T(8,128)(2,1)} %param.9) | data formatting | bytes 2949120 | tf_op args[0]
  7.8 0.0 copy-start.1
  7.8 1.7 %copy.29 = bf16[8,360,4,64]{1,3,0,2:T(8,128)(2,1)S(1)} copy(bf16[8,360,4,64]{1,3,2,0:T(8,128)(2,1)} %bitcast.27) | data formatting | bytes 2949120 | tf_op jit(solution)/shard_map/reshape;squeeze | solution.py:545
  9.6 0.4 copy-done.1
  10.0 0.0 copy-start.3
  10.0 1.4 %copy-done.3 = bf16[4,768,192]{2,1,0:T(8,128)(2,1)S(1)} copy-done((bf16[4,768,192]{2,1,0:T(8,128)(2,1)S(1)}, bf16[4,768,192]{2,1,0:T(8,128)(2,1)}, u32[]{:S(2)}) %copy-start.3) | copy-done | bytes 1179672
  11.4 0.0 copy-start.2
  11.4 0.0 copy-start.4
  11.4 39.1 %shard_map.112 = (bf16[4,768,256]{2,1,0:T(8,128)(2,1)S(1)}, bf16[4,8,64,360]{3,2,1,0:T(8,128)(2,1)S(1)}, bf16[4,8,64,360]{3,2,1,0:T(8,128)(2,1)S(1)}) custom-call(bf16[4,192,256]{2,1,0:T(8,128)(2,1)S(1)} %pad.10.refs_0_, bf16[4,8,64,360]{3,2,1,0:T(8,128)(2,1)S(1)} %bitcast.21, bf16[4,768,192]{2,1,0:T(8,128)(2,1)S(1)} %copy-done.3, ...), custom_call_target="tpu_custom_call" | custom-call | flops 20000000000 | bytes 10000000 | tf_op jit(solution)/shard_map/pallas_call | solution.py:237
  50.5 0.0 copy-done.2
  50.5 0.0 copy-done.4
  50.5 41.1 %shard_map.113 = (bf16[4,180,256]{2,1,0:T(8,128)(2,1)S(1)}, f32[576,256]{1,0:T(8,128)S(1)}, bf16[4,8,64,360]{3,2,1,0:T(8,128)(2,1)S(1)}) custom-call(bf16[4,8,64,360]{3,2,1,0:T(8,128)(2,1)S(1)} %get-tuple-element.9.refs_0_, bf16[4,8,64,360]{3,2,1,0:T(8,128)(2,1)S(1)} %get-tuple-element.10.refs_1_, bf16[4,360,768]{2,1,0:T(8,128)(2,1)S(1)} %copy-done.2, ...), custom_call_target="tpu_custom_call" | custom-call | flops 20000000000 | bytes 10000000 | tf_op jit(solution)/shard_map/pallas_call | solution.py:489
  91.6 0.9 copy.23
  92.5 1.3 %copy.22 = bf16[8,360,4,64]{1,3,2,0:T(8,128)(2,1)} copy(bf16[8,360,4,64]{1,3,0,2:T(8,128)(2,1)S(1)} %bitcast.20) | data formatting | bytes 2949120 | tf_op jit(solution)/shard_map/transpose | solution.py:566
  93.8 2.6 %copy.24 = bf16[1,8,360,256]{3,2,1,0:T(8,128)(2,1)} copy(bf16[1,8,360,256]{2,3,1,0:T(8,128)(2,1)} %bitcast.26) | data formatting | bytes 2949120
  96.4 0.8 copy.32
  (5 shorter events, 0.1 us)
Async XLA Ops:
  0.6 3.3 %copy-start = (bf16[9,256,256]{2,1,0:T(8,128)(2,1)S(1)}, bf16[9,256,256]{2,1,0:T(8,128)(2,1)}, u32[]{:S(2)}) copy-start(bf16[9,256,256]{2,1,0:T(8,128)(2,1)} %param.12) | copy-start | bytes 3538948
  1.5 2.7 %copy-start.6 = (bf16[1,4,180,256]{3,1,2,0:T(4,128)(2,1)S(1)}, bf16[1,4,180,256]{3,1,2,0:T(4,128)(2,1)}, u32[]{:S(2)}) copy-start(bf16[1,4,180,256]{3,1,2,0:T(4,128)(2,1)} %param.13) | copy-start | bytes 1105924
  4.1 1.0 %copy-start.5 = (bf16[9,4,10,360]{3,2,0,1:T(8,128)(2,1)S(1)}, bf16[9,4,10,360]{3,2,0,1:T(8,128)(2,1)}, u32[]{:S(2)}) copy-start(bf16[9,4,10,360]{3,2,0,1:T(8,128)(2,1)} %reshape.66) | copy-start | bytes 777604
  7.8 2.1 %copy-start.1 = (bf16[4,768,360]{2,1,0:T(8,128)(2,1)S(1)}, bf16[4,768,360]{2,1,0:T(8,128)(2,1)}, u32[]{:S(2)}) copy-start(bf16[4,768,360]{2,1,0:T(8,128)(2,1)} %constant.24.clone.refs_5_) | copy-start | bytes 6635524
  10.0 1.4 %copy-start.3 = (bf16[4,768,192]{2,1,0:T(8,128)(2,1)S(1)}, bf16[4,768,192]{2,1,0:T(8,128)(2,1)}, u32[]{:S(2)}) copy-start(bf16[4,768,192]{2,1,0:T(8,128)(2,1)} %constant.23.clone.refs_2_) | copy-start | bytes 3538948
  11.4 39.1 %copy-start.2 = (bf16[4,360,768]{2,1,0:T(8,128)(2,1)S(1)}, bf16[4,360,768]{2,1,0:T(8,128)(2,1)}, u32[]{:S(2)}) copy-start(bf16[4,360,768]{2,1,0:T(8,128)(2,1)} %constant.25.clone.refs_2_) | copy-start | bytes 6635524
  11.4 39.1 %copy-start.4 = (bf16[4,192,768]{2,1,0:T(8,128)(2,1)S(1)}, bf16[4,192,768]{2,1,0:T(8,128)(2,1)}, u32[]{:S(2)}) copy-start(bf16[4,192,768]{2,1,0:T(8,128)(2,1)} %constant.26.clone.refs_6_) | copy-start | bytes 3538948
